TPU v7x, 32 devices: a whole 2x2x4 slice. The times are simulated.
32 devices in a mesh: groups: 2 (over y), adapt: 16 (over z, x, core).
Axes of the slice: x: 2, y: 2, z: 4, core: 2. Of those that a mesh axis runs over, the one named last changes fastest.
Arguments:
- tokens: bfloat16 [256, 8192], P(('groups', 'adapt')), parts along dimension 0, may hold values from -6 to 6
- up_weight: bfloat16 [8192, 28672], P(None, 'adapt'), may hold values from -0.0625 to 0.0625
- adapter_down_weight: bfloat16 [16, 8192, 64], P('adapt'), may hold values from -0.0625 to 0.0625
- adapter_up_weight: bfloat16 [16, 64, 28672], P('adapt'), may hold values from -0.75 to 0.75
- adapter_scale_values: float32 [16], P('adapt'), may hold values from 0.25 to 2
- row_adapter_index: int32 [256, 1], P('groups'), parts along dimension 0, may hold values from 0 to 15; in each aligned block of 128 rows (0 to 127, 128 to 255, ...) at most 16 rows name the same one
Outputs:
- up_out: bfloat16 [256, 28672], P('groups', 'adapt'), parts along dimension 0
There are 2 independent parts, one for each index of `groups`. A program takes and returns all parts, laid end to end along the dimension named above; an argument that names none is the same for every part. Nothing has to cross between parts.
Inputs may be any that keep to these rules, and one draw needn't show every extreme that they name: `row_adapter_index`: every adapter is named by at least one row and at most 16 rows; some adapter by exactly 16.
All inputs are finite; a program needn't handle non-finite values.
Results may differ from a plain program's by a relative error of at most 0.0052.
Values may be sent and summed in bfloat16 or wider, within the bound.
No kernel may reach another device: no remote copies, remote signals or barrier semaphores. Data moves between devices by JAX's collectives and lax.ppermute only.
A program may use at most 128 MiB of HBM per device.

v0:
```python
import jax
import jax.numpy as jnp
from jax import lax
from jax.sharding import PartitionSpec as P

CAP = 16


def body(
    tokens,
    up_weight,
    adapter_down_weight,
    adapter_up_weight,
    adapter_scale_values,
    row_adapter_index,
):
    dev_count = lax.axis_size("adapt")
    my_index = lax.axis_index("adapt")
    rows_per_shard = adapter_down_weight.shape[0]
    total_adapters = rows_per_shard * dev_count
    row_ids = row_adapter_index[:, 0]
    row_count = row_ids.shape[0]
    gathered = lax.all_gather(tokens, "adapt", axis=0, tiled=True)
    base_part = jnp.dot(gathered, up_weight, preferred_element_type=jnp.float32)
    matches = (row_ids[:, None] == jnp.arange(total_adapters, dtype=jnp.int32)[None, :]).astype(
        jnp.int32
    )
    running = jnp.cumsum(matches, axis=0)
    row_rank = jnp.sum(matches * running, axis=1) - 1
    owned = my_index * rows_per_shard + jnp.arange(rows_per_shard, dtype=jnp.int32)
    positions = jnp.arange(CAP, dtype=jnp.int32)
    select = (row_ids[None, None, :] == owned[:, None, None]) & (
        row_rank[None, None, :] == positions[None, :, None]
    )
    slot_rows = jnp.sum(
        jnp.where(select, jnp.arange(row_count, dtype=jnp.int32)[None, None, :], 0), axis=2
    )
    completed_output = jnp.any(select, axis=2)
    selected_weight = jnp.take(gathered, slot_rows, axis=0)
    rank_output = jnp.einsum(
        "qeb,qbo->qeo", selected_weight, adapter_down_weight, preferred_element_type=jnp.float32
    )
    adapter_scale = jnp.where(
        completed_output[:, :, None], rank_output * adapter_scale_values[:, None, None], 0.0
    ).astype(jnp.bfloat16)
    widened_output = jnp.einsum(
        "jck,jkf->jcf", adapter_scale, adapter_up_weight, preferred_element_type=jnp.float32
    ).astype(jnp.bfloat16)
    arrived = lax.all_to_all(
        widened_output.reshape(rows_per_shard * CAP, -1),
        "adapt",
        split_axis=1,
        concat_axis=0,
        tiled=True,
    )
    deltas = jnp.take(arrived, row_ids * CAP + row_rank, axis=0)
    return (base_part + deltas.astype(jnp.float32)).astype(jnp.bfloat16)


def solution(mesh):
    placed = (
        P(("groups", "adapt"), None),
        P(None, "adapt"),
        P("adapt", None, None),
        P("adapt", None, None),
        P("adapt"),
        P("groups", None),
    )
    return jax.shard_map(
        body, mesh=mesh, in_specs=placed, out_specs=P("groups", "adapt"), check_vma=False
    )
```

profile of v0, /device:TPU:9, one launch (start us, length us, event | category | flops | bytes accessed | tf_op | source)
XLA Modules:
  0.0 108.6 jit_solution(2251469603582593261)
XLA Ops:
  6.5 0.0 copy-start
  6.5 0.0 all-gather.2.cloned.1.call-start
  6.5 0.7 all-gather.2.cloned.1.call-update
  7.9 0.7 fusion.12
  8.7 0.2 reduce_window_sum.11
  8.8 0.8 select_reduce_fusion
  9.7 0.7 broadcast_compare_fusion
  10.3 0.1 select_reduce_fusion.1
  10.5 0.1 fusion.14
  10.6 41.0 %all-gather.2.cloned.1.call-done = bf16[128,8192]{1,0:T(8,128)(2,1)} async-done(((bf16[8,8192]{1,0:T(8,128)(2,1)}), bf16[128,8192]{1,0:T(8,128)(2,1)}) %all-gather.2.cloned.1.call-update) | async-done | bytes 2097168 | tf_op jit(solution)/shard_map/all_gather | solution.py:23
  51.6 2.8 %gather_fusion = bf16[16,8192]{1,0:T(8,128)(2,1)S(1)} fusion(bf16[128,8192]{1,0:T(8,128)(2,1)} %all-gather.2.cloned.1.call-done, s32[1024]{0:T(1024)S(1)} %pad_clamp_fusion.1), kind=kCustom, calls=%fused_computation | custom fusion | bytes 524352 | tf_op jit(solution)/shard_map/jit(_take)/gather | solution.py:39
  54.4 0.0 copy-done
  54.4 0.0 copy-start.1
  54.4 3.6 %convolution_convert_fusion = bf16[16,28672]{1,0:T(8,128)(2,1)S(1)} fusion(bf16[1,64,28672]{2,1,0:T(8,128)(2,1)} %param.9, bf16[1,8192,64]{1,2,0:T(8,128)(2,1)S(1)} %copy-done, bf16[16,8192]{1,0:T(8,128)(2,1)S(1)} %gather_fusion, pred[16]{0:T(512)(128)(4,1)S(1)} %compare_and_fusion, f32[]{:T(128)} %bitcast.41, pred[16]{0:T(512)(128)(4,1)S(1)} %fusion.14), kind=kOutput, calls=%fused_computation.2 | convolution fusion | flops 76090368 | bytes 5898276 | tf_op jit(solution)/shard_map/jck,jkf->jcf/dot_general | solution.py:46
  58.0 1.0 copy.12
  59.0 4.8 %all-to-all-start = ((bf16[16,16,1792]{2,0,1:T(8,128)(2,1)}), bf16[16,16,1792]{2,0,1:T(8,128)(2,1)S(1)}, u32[]{:S(2)}, u32[]{:S(2)}) async-start(bf16[16,16,1792]{2,0,1:T(8,128)(2,1)} %bitcast.40), calls=%async_computation | async-start | bytes 1835008 | tf_op jit(solution)/shard_map/all_to_all | solution.py:49
  63.9 0.0 copy-done.1
  63.9 22.2 %all-to-all-done = bf16[16,16,1792]{2,0,1:T(8,128)(2,1)S(1)} async-done(((bf16[16,16,1792]{2,0,1:T(8,128)(2,1)}), bf16[16,16,1792]{2,0,1:T(8,128)(2,1)S(1)}, u32[]{:S(2)}, u32[]{:S(2)}) %all-to-all-start) | async-done | bytes 917536 | tf_op jit(solution)/shard_map/all_to_all | solution.py:49
  86.1 0.9 gather_fusion.1
  87.0 14.7 %fusion.1 = bf16[128,1792]{1,0:T(8,128)(2,1)} fusion(bf16[128,8192]{1,0:T(8,128)(2,1)} %all-gather.2.cloned.1.call-done, bf16[8192,1792]{1,0:T(8,128)(2,1)} %param.7, bf16[128,1792]{1,0:T(8,128)(2,1)S(1)} %gather_fusion.1, pred[128]{0:T(512)(128)(4,1)S(1)} %get-tuple-element.5), kind=kOutput, calls=%fused_computation.5 | convolution fusion | flops 3759013888 | bytes 32374912 | tf_op jit(solution)/shard_map/dot_general | solution.py:24
  (6 shorter events, 0.0 us)
Async XLA Ops:
  6.5 47.9 %copy-start = (bf16[1,8192,64]{1,2,0:T(8,128)(2,1)S(1)}, bf16[1,8192,64]{1,2,0:T(8,128)(2,1)}, u32[]{:S(2)}) copy-start(bf16[1,8192,64]{1,2,0:T(8,128)(2,1)} %param.8) | copy-start | bytes 3145732
  6.5 45.0 %all-gather.2.cloned.1.call-start = ((), (), s32[]{:S(2)}) async-start(), calls=%async_computation.1 | async-start | bytes 2228224 | tf_op jit(solution)/shard_map/all_gather | solution.py:23
  54.4 9.5 %copy-start.1 = (s32[128,1]{0,1:T(1,128)S(1)}, s32[128,1]{0,1:T(1,128)}, u32[]{:S(2)}) copy-start(s32[128,1]{0,1:T(1,128)} %param.11) | copy-start | bytes 1540
  59.0 27.1 %all-to-all-start = ((bf16[16,16,1792]{2,0,1:T(8,128)(2,1)}), bf16[16,16,1792]{2,0,1:T(8,128)(2,1)S(1)}, u32[]{:S(2)}, u32[]{:S(2)}) async-start(bf16[16,16,1792]{2,0,1:T(8,128)(2,1)} %bitcast.40), calls=%async_computation | async-start | bytes 1835008 | tf_op jit(solution)/shard_map/all_to_all | solution.py:49
Sparse Core Ops, SparseCore 0:
  9.5 42.0 all-gather.1
where the time goes:
time: 109 us
  waiting for transfers between devices  63.9 us (59%)
  matrix products  18.3 us (17%)
  between operations  14.1 us (13%)
  starting transfers between devices  4.84 us (4%)
  local copies, waits for them, and re-layouts  4.75 us (4%)
  other arithmetic  2.68 us (2%)
    all_gather x1, waiting for transfers between devices, body(): gathered = lax.all_gather(tokens, 'adapt', axis=0, tiled=True)  41 us
    all_to_all x1, waiting for transfers between devices, body(): lax.all_to_all(widened_output.reshape(rows_per_shard * CAP, -1), 'adapt',...  22.2 us
    dot_general x1, matrix products, body(): base_part = jnp.dot(gathered, up_weight, preferred_element_type=jnp.float32)  14.7 us
    all_to_all x1, starting transfers between devices, body(): lax.all_to_all(widened_output.reshape(rows_per_shard * CAP, -1), 'adapt',...  4.84 us
    dot_general x1, matrix products, body(): jnp.einsum('jck,jkf->jcf', adapter_scale, adapter_up_weight, preferred_el...  3.61 us
    gather x1, local copies, waits for them, and re-layouts, body(): selected_weight = jnp.take(gathered, slot_rows, axis=0)  2.8 us
  transfers between devices with their start and end apart: 2, of which 2 were waited for; matrix products, arithmetic and copies ran while one was open for 2% of the time, Pallas kernels for 0%

commit v1 on v0

v1 whole, which is shorter than its diff:
```python
import functools

import jax
import jax.numpy as jnp
from jax import lax
from jax.experimental import pallas as pl
from jax.experimental.pallas import tpu as pltpu
from jax.sharding import PartitionSpec as P

CAP = 16
AXIS = "adapt"
MIB = 1 << 20


def swap(x, mask, count):
    return lax.ppermute(x, AXIS, [(i, i ^ mask) for i in range(count)])


def gather_chunks(x, count):
    near = min(4, count)
    chunks = {0: x}
    for far in range(near, count, near):
        chunks[far] = swap(x, far, count)
    for mask in (2, 1):
        if mask < near:
            for key in sorted(chunks):
                chunks[key ^ mask] = swap(chunks[key], mask, count)
    return [chunks[m] for m in range(count)]


def delta_kernel(scale_ref, owned_ref, ids_ref, rank_ref, x_ref, down_ref, up_ref, out_ref):
    low = lax.dot_general(
        x_ref[...], down_ref[...], (((1,), (1,)), ((), ())), preferred_element_type=jnp.float32
    )
    low = (low * scale_ref[0]).astype(jnp.bfloat16)
    slots = lax.broadcasted_iota(jnp.int32, (CAP, low.shape[0]), 0)
    pick = (ids_ref[...] == owned_ref[0]) & (rank_ref[...] == slots)
    pick = jnp.where(pick, 1.0, 0.0).astype(jnp.bfloat16)
    low = jnp.dot(pick, low, preferred_element_type=jnp.float32).astype(jnp.bfloat16)
    width = out_ref.shape[2]
    for j in range(out_ref.shape[0]):
        out_ref[j] = jnp.dot(
            low, up_ref[:, j * width : (j + 1) * width], preferred_element_type=jnp.float32
        ).astype(jnp.bfloat16)


def make_delta(x, down, up, scale, owned, ids, rank, count):
    hidden = up.shape[1]
    width = hidden // count
    vmem = pl.BlockSpec(memory_space=pltpu.VMEM)
    smem = pl.BlockSpec(memory_space=pltpu.SMEM)
    out = jax.ShapeDtypeStruct((count, CAP, width), jnp.bfloat16)
    if width % 128:
        low = (jnp.dot(x, down.T, preferred_element_type=jnp.float32) * scale[0]).astype(jnp.bfloat16)
        pick = (ids == owned[0]) & (rank == jnp.arange(CAP, dtype=jnp.int32)[:, None])
        low = jnp.dot(pick.astype(jnp.bfloat16), low, preferred_element_type=jnp.float32)
        delta = jnp.dot(low.astype(jnp.bfloat16), up, preferred_element_type=jnp.float32)
        return delta.astype(jnp.bfloat16).reshape(CAP, count, width).transpose(1, 0, 2)
    return pl.pallas_call(
        delta_kernel,
        out_shape=out,
        in_specs=[smem, smem, vmem, vmem, vmem, vmem, vmem],
        out_specs=vmem,
        compiler_params=pltpu.CompilerParams(vmem_limit_bytes=24 * MIB),
        cost_estimate=pl.CostEstimate(
            flops=2 * x.size * 64, bytes_accessed=2 * (x.size + down.size + up.size), transcendentals=0
        ),
    )(scale, owned, ids, rank, x, down, up)


def combine_kernel(rows_each, me_ref, slot_ref, base_ref, arrived_ref, out_ref, acc):
    rows = base_ref.shape[0]
    for m in range(rows // rows_each):
        at = pl.multiple_of((me_ref[0] ^ m) * rows_each, rows_each)
        acc[pl.ds(at, rows_each), :] = base_ref[m * rows_each : (m + 1) * rows_each, :]
    places = lax.broadcasted_iota(jnp.int32, (rows, arrived_ref.shape[0]), 1)
    pick = jnp.where(slot_ref[...] == places, 1.0, 0.0).astype(jnp.bfloat16)
    delta = jnp.dot(pick, arrived_ref[...], preferred_element_type=jnp.float32)
    out_ref[...] = (acc[...] + delta).astype(jnp.bfloat16)


def combine(base, arrived, slot, me, rows_each):
    rows, width = base.shape
    vmem = pl.BlockSpec(memory_space=pltpu.VMEM)
    smem = pl.BlockSpec(memory_space=pltpu.SMEM)
    return pl.pallas_call(
        functools.partial(combine_kernel, rows_each),
        out_shape=jax.ShapeDtypeStruct((rows, width), jnp.bfloat16),
        in_specs=[smem, vmem, vmem, vmem],
        out_specs=vmem,
        scratch_shapes=[pltpu.VMEM((rows, width), jnp.float32)],
        compiler_params=pltpu.CompilerParams(vmem_limit_bytes=24 * MIB),
        cost_estimate=pl.CostEstimate(
            flops=2 * rows * arrived.size, bytes_accessed=4 * base.size, transcendentals=0
        ),
    )(me, slot, base, arrived)


def body(count, tokens, up_weight, down, up, scale, row_index):
    me = lax.axis_index(AXIS)
    rows_each = tokens.shape[0]
    ids = row_index[:, 0]
    rows = ids.shape[0]
    adapters = down.shape[0] * count
    matches = (ids[:, None] == jnp.arange(adapters, dtype=jnp.int32)[None, :]).astype(jnp.int32)
    running = jnp.cumsum(matches, axis=0)
    rank = jnp.sum(matches * running, axis=1) - 1
    slot = (ids * CAP + rank)[:, None]
    place = jnp.arange(rows, dtype=jnp.int32)
    place = ((place // rows_each) ^ me) * rows_each + place % rows_each
    ids_here, rank_here = ids[place], rank[place]
    me = me.astype(jnp.int32)[None]

    x = jnp.concatenate(gather_chunks(tokens, count), axis=0)
    delta = make_delta(
        x,
        jnp.swapaxes(down[0], 0, 1),
        up[0],
        scale,
        me,
        ids_here[None, :],
        rank_here[None, :],
        count,
    )
    arrived = lax.all_to_all(delta, AXIS, split_axis=0, concat_axis=0, tiled=True)
    base = jnp.dot(x, up_weight, preferred_element_type=jnp.float32)
    return combine(base, arrived.reshape(count * CAP, -1), slot, me, rows_each)


def solution(mesh):
    placed = (
        P(("groups", AXIS), None),
        P(None, AXIS),
        P(AXIS, None, None),
        P(AXIS, None, None),
        P(AXIS),
        P("groups", None),
    )
    return jax.shard_map(
        functools.partial(body, mesh.shape[AXIS]),
        mesh=mesh,
        in_specs=placed,
        out_specs=P("groups", AXIS),
        check_vma=False,
    )
```

time: 109 us -> 60.6 us (0.56)
  waiting for transfers between devices: 63.9 us -> 13.5 us
  starting transfers between devices: 4.84 us -> 18.6 us
  between operations: 14.1 us -> 0.9 us
  matrix products: 18.3 us -> 12.4 us
  local copies, waits for them, and re-layouts: 4.75 us -> 9.02 us
  Pallas kernels: 0 us -> 3.44 us
    all_gather x1 -> x0, waiting for transfers between devices: 41 us -> none  [body(): gathered = lax.all_gather(tokens, 'adapt', axis=0, tiled=True)]
    ppermute x0 -> x15, starting transfers between devices: none -> 12.9 us  [swap(): return lax.ppermute(x, AXIS, [(i, i ^ mask) for i in range(count)])]
    all_to_all x1, waiting for transfers between devices: 22.2 us -> 9.81 us  [body(): lax.all_to_all(delta, AXIS, split_axis=0, concat_axis=0, tiled=True)]
    unnamed x4 -> x23, local copies, waits for them, and re-layouts: 0.01 us -> 5.99 us
    dot_general x2 -> x1, matrix products: 18.3 us -> 12.4 us  [body(): base = jnp.dot(x, up_weight, preferred_element_type=jnp.float32)]
    ppermute x0 -> x15, waiting for transfers between devices: none -> 3.74 us  [swap(): return lax.ppermute(x, AXIS, [(i, i ^ mask) for i in range(count)])]
    pallas_call x0 -> x2, Pallas kernels: none -> 3.44 us  [the longest x1 2.31 us: make_delta(): pl.pallas_call(delta_kernel, out_shape=out, in_specs=[smem, smem, vmem, v...]
  transfers between devices with their start and end apart: 2 -> 16, of which waited for: 2 -> 4; matrix products, arithmetic and copies ran while one was open for 2% -> 36% of each run, Pallas kernels for 0% -> 0%
where the time goes in v1:
time: 60.6 us; the launch traced here: 60.3 us
  starting transfers between devices  18.6 us (31%)
  waiting for transfers between devices  13.5 us (22%)
  matrix products  12.4 us (20%)
  local copies, waits for them, and re-layouts  9.02 us (15%)
  Pallas kernels  3.44 us (6%)
  other arithmetic  2.42 us (4%)
  between operations  0.9 us (1%)
    ppermute x15, starting transfers between devices, swap(): return lax.ppermute(x, AXIS, [(i, i ^ mask) for i in range(count)])  12.9 us
    dot_general x1, matrix products, body(): base = jnp.dot(x, up_weight, preferred_element_type=jnp.float32)  12.4 us
    all_to_all x1, waiting for transfers between devices, body(): lax.all_to_all(delta, AXIS, split_axis=0, concat_axis=0, tiled=True)  9.81 us
    unnamed x23, local copies, waits for them, and re-layouts  5.99 us
    all_to_all x1, starting transfers between devices, body(): lax.all_to_all(delta, AXIS, split_axis=0, concat_axis=0, tiled=True)  5.69 us
    ppermute x15, waiting for transfers between devices, swap(): return lax.ppermute(x, AXIS, [(i, i ^ mask) for i in range(count)])  3.74 us
    gather x2, local copies, waits for them, and re-layouts, body(): ids_here, rank_here = (ids[place], rank[place])  2.9 us
    pallas_call x1, Pallas kernels, make_delta(): pl.pallas_call(delta_kernel, out_shape=out, in_specs=[smem, smem, vmem, v...  2.31 us
  transfers between devices with their start and end apart: 16, of which 4 were waited for; matrix products, arithmetic and copies ran while one was open for 36% of the time, Pallas kernels for 0%

profile of v1, /device:TPU:9, one launch (start us, length us, event | category | flops | bytes accessed | tf_op | source)
XLA Modules:
  0.0 60.3 jit_solution(16481478579341266027)
XLA Ops:
  0.0 1.2 %collective-permute-start.1 = (bf16[8,8192]{1,0:T(8,128)(2,1)}, bf16[8,8192]{1,0:T(8,128)(2,1)}, u32[]{:S(2)}, u32[]{:S(2)}) collective-permute-start(bf16[8,8192]{1,0:T(8,128)(2,1)} %param.6), channel_id=1, source_target_pairs={{0,2},{1,3},{2,0},{3,1},{4,6},{5,7},{6,4},{7,5},{8,10},{9,11},{10,... | collective-permute-start | bytes 393224 | tf_op jit(solution)/shard_map/ppermute | solution.py:16
  1.2 1.0 %collective-permute-start = (bf16[8,8192]{1,0:T(8,128)(2,1)}, bf16[8,8192]{1,0:T(8,128)(2,1)}, u32[]{:S(2)}, u32[]{:S(2)}) collective-permute-start(bf16[8,8192]{1,0:T(8,128)(2,1)} %param.6), channel_id=1, source_target_pairs={{0,1},{1,0},{2,3},{3,2},{4,5},{5,4},{6,7},{7,6},{8,9},{9,8},{10,11... | collective-permute-start | bytes 393224 | tf_op jit(solution)/shard_map/ppermute | solution.py:16
  2.2 0.2 collective-permute-start.3
  2.3 2.3 %collective-permute-start.7 = (bf16[8,8192]{1,0:T(8,128)(2,1)}, bf16[8,8192]{1,0:T(8,128)(2,1)S(1)}, u32[]{:S(2)}, u32[]{:S(2)}) collective-permute-start(bf16[8,8192]{1,0:T(8,128)(2,1)} %param.6), channel_id=1, source_target_pairs={{0,8},{1,9},{2,10},{3,11},{4,12},{5,13},{6,14},{7,15},{8,0},{9,1},... | collective-permute-start | bytes 393224 | tf_op jit(solution)/shard_map/ppermute | solution.py:16
  4.6 0.2 collective-permute-start.11
  4.8 0.9 %constant_dynamic-update-slice_fusion.15 = bf16[128,8192]{1,0:T(8,128)(2,1)S(1)} fusion(bf16[8,8192]{1,0:T(8,128)(2,1)} %param.6), kind=kLoop, calls=%fused_computation.20 | loop fusion | bytes 262144
  5.8 0.7 %fusion = s32[128,16]{1,0:T(8,128)S(1)} fusion(s32[128]{0:T(128)} %bitcast.20), kind=kLoop, calls=%fused_computation.4 | loop fusion | flops 4096 | bytes 8704 | tf_op jit(solution)/shard_map/convert_element_type | solution.py:105
  6.5 0.2 reduce_window_sum.11
  6.7 0.8 %select_reduce_fusion = s32[128]{0:T(128)S(1)} fusion(s32[128,16]{1,0:T(8,128)S(1)} %reduce_window_sum.11, s32[128]{0:T(128)} %bitcast.21), kind=kLoop, calls=%fused_computation.2 | loop fusion | flops 6016 | bytes 9216 | tf_op jit(solution)/shard_map/reduce_sum | solution.py:107
  7.6 0.0 copy-start.3
  7.6 1.7 %gather_fusion = s32[128]{0:T(128)S(1)} fusion(s32[128]{0:T(128)} %bitcast.22, s32[1024]{0:T(1024)S(1)} %pad_clamp_fusion), kind=kCustom, calls=%fused_computation | custom fusion | bytes 1536 | tf_op jit(solution)/shard_map/gather | solution.py:111
  9.2 1.2 %gather_fusion.1 = s32[128]{0:T(128)S(1)} fusion(s32[128]{0:T(128)S(1)} %broadcast_add_fusion, s32[1024]{0:T(1024)S(1)} %pad_clamp_fusion), kind=kCustom, calls=%fused_computation.1 | custom fusion | bytes 1536 | tf_op jit(solution)/shard_map/gather | solution.py:111
  11.1 0.7 %bitcast_add_fusion = s32[128,1]{0,1:T(1,128)S(1)} fusion(s32[128,1]{0,1:T(1,128)} %param.11, s32[128]{0:T(128)S(1)} %select_reduce_fusion), kind=kLoop, calls=%fused_computation.32 | loop fusion | flops 384 | bytes 1536 | tf_op jit(solution)/shard_map/add | solution.py:108
  11.8 0.1 copy.13.slot_ref
  11.9 0.0 collective-permute-done.3
  11.9 0.9 %collective-permute-start.4 = (bf16[8,8192]{1,0:T(8,128)(2,1)}, bf16[8,8192]{1,0:T(8,128)(2,1)S(1)}, u32[]{:S(2)}, u32[]{:S(2)}) collective-permute-start(bf16[8,8192]{1,0:T(8,128)(2,1)} %collective-permute-done.3), channel_id=1, source_target_pairs={{0,1},{1,0},{2,3},{3,2},{4,5},{5,4},{6,7},{7,6},{8,9},{9,8},{10,11... | collective-permute-start | bytes 393224 | tf_op jit(solution)/shard_map/ppermute | solution.py:16
  12.8 0.0 collective-permute-done.1
  12.8 0.3 collective-permute-start.5
  13.1 0.0 collective-permute-done
  13.1 0.4 collective-permute-start.2
  13.5 0.9 %constant_dynamic-update-slice_fusion.14 = bf16[128,8192]{1,0:T(8,128)(2,1)S(1)} fusion(bf16[128,8192]{1,0:T(8,128)(2,1)S(1)} %constant_dynamic-update-slice_fusion.15, bf16[8,8192]{1,0:T(8,128)(2,1)} %collective-permute-done), kind=kLoop, calls=%fused_computation.19 | loop fusion | bytes 262144
  14.4 0.9 %constant_dynamic-update-slice_fusion.13 = bf16[128,8192]{1,0:T(8,128)(2,1)S(1)} fusion(bf16[128,8192]{1,0:T(8,128)(2,1)S(1)} %constant_dynamic-update-slice_fusion.14, bf16[8,8192]{1,0:T(8,128)(2,1)} %collective-permute-done.1), kind=kLoop, calls=%fused_computation.18 | loop fusion | bytes 262144
  15.3 0.0 collective-permute-done.7
  15.3 0.5 collective-permute-start.8
  15.8 1.1 %collective-permute-done.11 = bf16[8,8192]{1,0:T(8,128)(2,1)S(1)} collective-permute-done((bf16[8,8192]{1,0:T(8,128)(2,1)}, bf16[8,8192]{1,0:T(8,128)(2,1)S(1)}, u32[]{:S(2)}, u32[]{:S(2)}) %collective-permute-start.11) | collective-permute-done | bytes 131104 | tf_op jit(solution)/shard_map/ppermute | solution.py:16
  16.9 0.3 collective-permute-start.9
  17.1 0.0 collective-permute-done.2
  17.1 1.4 %collective-permute-start.12 = (bf16[8,8192]{1,0:T(8,128)(2,1)S(1)}, bf16[8,8192]{1,0:T(8,128)(2,1)S(1)}, u32[]{:S(2)}, u32[]{:S(2)}) collective-permute-start(bf16[8,8192]{1,0:T(8,128)(2,1)S(1)} %collective-permute-done.11), channel_id=1, source_target_pairs={{0,1},{1,0},{2,3},{3,2},{4,5},{5,4},{6,7},{7,6},{8,9},{9,8},{10,11... | collective-permute-start | bytes 393224 | tf_op jit(solution)/shard_map/ppermute | solution.py:16
  18.5 0.9 %constant_dynamic-update-slice_fusion.11 = bf16[128,8192]{1,0:T(8,128)(2,1)S(1)} fusion(bf16[128,8192]{1,0:T(8,128)(2,1)S(1)} %constant_dynamic-update-slice_fusion.12, bf16[8,8192]{1,0:T(8,128)(2,1)} %collective-permute-done.3), kind=kLoop, calls=%fused_computation.16 | loop fusion | bytes 262144
  19.4 0.0 collective-permute-done.4
  19.4 1.3 %collective-permute-start.13 = (bf16[8,8192]{1,0:T(8,128)(2,1)S(1)}, bf16[8,8192]{1,0:T(8,128)(2,1)S(1)}, u32[]{:S(2)}, u32[]{:S(2)}) collective-permute-start(bf16[8,8192]{1,0:T(8,128)(2,1)S(1)} %collective-permute-done.11), channel_id=1, source_target_pairs={{0,2},{1,3},{2,0},{3,1},{4,6},{5,7},{6,4},{7,5},{8,10},{9,11},{10,... | collective-permute-start | bytes 393224 | tf_op jit(solution)/shard_map/ppermute | solution.py:16
  20.7 0.0 collective-permute-done.5
  20.7 0.3 collective-permute-start.6
  21.0 0.0 collective-permute-done.9
  21.1 2.2 %collective-permute-start.10 = (bf16[8,8192]{1,0:T(8,128)(2,1)S(1)}, bf16[8,8192]{1,0:T(8,128)(2,1)S(1)}, u32[]{:S(2)}, u32[]{:S(2)}) collective-permute-start(bf16[8,8192]{1,0:T(8,128)(2,1)S(1)} %collective-permute-done.9), channel_id=1, source_target_pairs={{0,1},{1,0},{2,3},{3,2},{4,5},{5,4},{6,7},{7,6},{8,9},{9,8},{10,11... | collective-permute-start | bytes 393224 | tf_op jit(solution)/shard_map/ppermute | solution.py:16
  23.2 1.8 %collective-permute-done.13 = bf16[8,8192]{1,0:T(8,128)(2,1)S(1)} collective-permute-done((bf16[8,8192]{1,0:T(8,128)(2,1)S(1)}, bf16[8,8192]{1,0:T(8,128)(2,1)S(1)}, u32[]{:S(2)}, u32[]{:S(2)}) %collective-permute-start.13) | collective-permute-done | bytes 131104 | tf_op jit(solution)/shard_map/ppermute | solution.py:16
  25.0 0.7 %collective-permute-start.14 = (bf16[8,8192]{1,0:T(8,128)(2,1)S(1)}, bf16[8,8192]{1,0:T(8,128)(2,1)S(1)}, u32[]{:S(2)}, u32[]{:S(2)}) collective-permute-start(bf16[8,8192]{1,0:T(8,128)(2,1)S(1)} %collective-permute-done.13), channel_id=1, source_target_pairs={{0,1},{1,0},{2,3},{3,2},{4,5},{5,4},{6,7},{7,6},{8,9},{9,8},{10,11... | collective-permute-start | bytes 393224 | tf_op jit(solution)/shard_map/ppermute | solution.py:16
  25.8 0.0 collective-permute-done.8
  25.8 0.0 collective-permute-done.10
  25.9 0.0 collective-permute-done.12
  25.9 0.8 %collective-permute-done.14 = bf16[8,8192]{1,0:T(8,128)(2,1)S(1)} collective-permute-done((bf16[8,8192]{1,0:T(8,128)(2,1)S(1)}, bf16[8,8192]{1,0:T(8,128)(2,1)S(1)}, u32[]{:S(2)}, u32[]{:S(2)}) %collective-permute-start.14) | collective-permute-done | bytes 131104 | tf_op jit(solution)/shard_map/ppermute | solution.py:16
  26.8 2.3 %shard_map.64 = bf16[16,16,1792]{2,1,0:T(8,128)(2,1)S(1)} custom-call(f32[1]{0:T(128)S(6)} %copy.29.scale_ref, s32[1]{0:T(128)} %bitcast.owned_ref.me_ref, s32[1,128]{1,0:T(1,128)S(1)} %bitcast.18, s32[1,128]{1,0:T(1,128)S(1)} %bitcast.19, bf16[128,8192]{1,0:T(8,128)(2,1)S(1)} %constant_dynamic-update-slice_fusion.x_ref, bf16[64,8192]{1,0:T(8,128)(2,1)S(1)} %bitcast.17, ...), custom_call_target="tpu_custom_call" | custom-call | flops 134217728 | bytes 6815744 | tf_op jit(solution)/shard_map/pallas_call | solution.py:59
  29.1 1.0 %copy-done.2 = bf16[16,16,1792]{2,1,0:T(8,128)(2,1)} copy-done((bf16[16,16,1792]{2,1,0:T(8,128)(2,1)}, bf16[16,16,1792]{2,1,0:T(8,128)(2,1)S(1)}, u32[]{:S(2)}) %copy-start.2) | copy-done | bytes 917528
  30.1 5.7 %all-to-all-start = ((bf16[16,16,1792]{2,1,0:T(8,128)(2,1)}), bf16[16,16,1792]{2,1,0:T(8,128)(2,1)S(1)}, u32[]{:S(2)}, u32[]{:S(2)}) async-start(bf16[16,16,1792]{2,1,0:T(8,128)(2,1)} %copy-done.2), calls=%async_computation | async-start | bytes 1835008 | tf_op jit(solution)/shard_map/all_to_all | solution.py:125
  35.8 12.4 %fusion.5.base_ref = f32[128,1792]{1,0:T(8,128)} fusion(bf16[128,8192]{1,0:T(8,128)(2,1)S(1)} %constant_dynamic-update-slice_fusion.x_ref, bf16[8192,1792]{1,0:T(8,128)(2,1)} %param.7), kind=kOutput, calls=%fused_computation.34 | convolution fusion | flops 3758096384 | bytes 32374784 | tf_op jit(solution)/shard_map/dot_general | solution.py:126
  48.2 9.8 %all-to-all-done = bf16[16,16,1792]{2,1,0:T(8,128)(2,1)S(1)} async-done(((bf16[16,16,1792]{2,1,0:T(8,128)(2,1)}), bf16[16,16,1792]{2,1,0:T(8,128)(2,1)S(1)}, u32[]{:S(2)}, u32[]{:S(2)}) %all-to-all-start) | async-done | bytes 917536 | tf_op jit(solution)/shard_map/all_to_all | solution.py:125
  58.0 1.2 %copy-done.1 = f32[128,1792]{1,0:T(8,128)S(1)} copy-done((f32[128,1792]{1,0:T(8,128)S(1)}, f32[128,1792]{1,0:T(8,128)}, u32[]{:S(2)}) %copy-start.1) | copy-done | bytes 917528
  59.1 1.1 %shard_map.65 = bf16[128,1792]{1,0:T(8,128)(2,1)} custom-call(s32[1]{0:T(128)} %bitcast.owned_ref.me_ref, s32[128,1]{1,0:T(8,128)S(1)} %copy.13.slot_ref, f32[128,1792]{1,0:T(8,128)S(1)} %copy-done.1, bf16[256,1792]{1,0:T(8,128)(2,1)S(1)} %bitcast.15), custom_call_target="tpu_custom_call" | custom-call | flops 117440512 | bytes 917504 | tf_op jit(solution)/shard_map/pallas_call | solution.py:86
  (21 shorter events, 0.2 us)
Async XLA Ops:
  0.0 12.8 %collective-permute-start.1 = (bf16[8,8192]{1,0:T(8,128)(2,1)}, bf16[8,8192]{1,0:T(8,128)(2,1)}, u32[]{:S(2)}, u32[]{:S(2)}) collective-permute-start(bf16[8,8192]{1,0:T(8,128)(2,1)} %param.6), channel_id=1, source_target_pairs={{0,2},{1,3},{2,0},{3,1},{4,6},{5,7},{6,4},{7,5},{8,10},{9,11},{10,... | collective-permute-start | bytes 393224 | tf_op jit(solution)/shard_map/ppermute | solution.py:16
  1.2 11.9 %collective-permute-start = (bf16[8,8192]{1,0:T(8,128)(2,1)}, bf16[8,8192]{1,0:T(8,128)(2,1)}, u32[]{:S(2)}, u32[]{:S(2)}) collective-permute-start(bf16[8,8192]{1,0:T(8,128)(2,1)} %param.6), channel_id=1, source_target_pairs={{0,1},{1,0},{2,3},{3,2},{4,5},{5,4},{6,7},{7,6},{8,9},{9,8},{10,11... | collective-permute-start | bytes 393224 | tf_op jit(solution)/shard_map/ppermute | solution.py:16
  2.2 9.8 %collective-permute-start.3 = (bf16[8,8192]{1,0:T(8,128)(2,1)}, bf16[8,8192]{1,0:T(8,128)(2,1)}, u32[]{:S(2)}, u32[]{:S(2)}) collective-permute-start(bf16[8,8192]{1,0:T(8,128)(2,1)} %param.6), channel_id=1, source_target_pairs={{0,4},{1,5},{2,6},{3,7},{4,0},{5,1},{6,2},{7,3},{8,12},{9,13},{10,... | collective-permute-start | bytes 393224 | tf_op jit(solution)/shard_map/ppermute | solution.py:16
  2.3 13.0 %collective-permute-start.7 = (bf16[8,8192]{1,0:T(8,128)(2,1)}, bf16[8,8192]{1,0:T(8,128)(2,1)S(1)}, u32[]{:S(2)}, u32[]{:S(2)}) collective-permute-start(bf16[8,8192]{1,0:T(8,128)(2,1)} %param.6), channel_id=1, source_target_pairs={{0,8},{1,9},{2,10},{3,11},{4,12},{5,13},{6,14},{7,15},{8,0},{9,1},... | collective-permute-start | bytes 393224 | tf_op jit(solution)/shard_map/ppermute | solution.py:16
  4.6 12.2 %collective-permute-start.11 = (bf16[8,8192]{1,0:T(8,128)(2,1)}, bf16[8,8192]{1,0:T(8,128)(2,1)S(1)}, u32[]{:S(2)}, u32[]{:S(2)}) collective-permute-start(bf16[8,8192]{1,0:T(8,128)(2,1)} %param.6), channel_id=1, source_target_pairs={{0,12},{1,13},{2,14},{3,15},{4,8},{5,9},{6,10},{7,11},{8,4},{9,5},... | collective-permute-start | bytes 393224 | tf_op jit(solution)/shard_map/ppermute | solution.py:16
  7.6 19.2 %copy-start.3 = (bf16[1,8192,64]{1,2,0:T(8,128)(2,1)S(1)}, bf16[1,8192,64]{1,2,0:T(8,128)(2,1)}, u32[]{:S(2)}) copy-start(bf16[1,8192,64]{1,2,0:T(8,128)(2,1)} %param.8) | copy-start | bytes 3145732
  11.9 14.8 %copy-start = (bf16[1,64,28672]{2,1,0:T(8,128)(2,1)S(1)}, bf16[1,64,28672]{2,1,0:T(8,128)(2,1)}, u32[]{:S(2)}) copy-start(bf16[1,64,28672]{2,1,0:T(8,128)(2,1)} %param.9) | copy-start | bytes 11010052
  11.9 7.5 %collective-permute-start.4 = (bf16[8,8192]{1,0:T(8,128)(2,1)}, bf16[8,8192]{1,0:T(8,128)(2,1)S(1)}, u32[]{:S(2)}, u32[]{:S(2)}) collective-permute-start(bf16[8,8192]{1,0:T(8,128)(2,1)} %collective-permute-done.3), channel_id=1, source_target_pairs={{0,1},{1,0},{2,3},{3,2},{4,5},{5,4},{6,7},{7,6},{8,9},{9,8},{10,11... | collective-permute-start | bytes 393224 | tf_op jit(solution)/shard_map/ppermute | solution.py:16
  12.8 7.9 %collective-permute-start.5 = (bf16[8,8192]{1,0:T(8,128)(2,1)}, bf16[8,8192]{1,0:T(8,128)(2,1)S(1)}, u32[]{:S(2)}, u32[]{:S(2)}) collective-permute-start(bf16[8,8192]{1,0:T(8,128)(2,1)} %collective-permute-done.3), channel_id=1, source_target_pairs={{0,2},{1,3},{2,0},{3,1},{4,6},{5,7},{6,4},{7,5},{8,10},{9,11},{10,... | collective-permute-start | bytes 393224 | tf_op jit(solution)/shard_map/ppermute | solution.py:16
  13.1 4.0 %collective-permute-start.2 = (bf16[8,8192]{1,0:T(8,128)(2,1)}, bf16[8,8192]{1,0:T(8,128)(2,1)S(1)}, u32[]{:S(2)}, u32[]{:S(2)}) collective-permute-start(bf16[8,8192]{1,0:T(8,128)(2,1)} %collective-permute-done.1), channel_id=1, source_target_pairs={{0,1},{1,0},{2,3},{3,2},{4,5},{5,4},{6,7},{7,6},{8,9},{9,8},{10,11... | collective-permute-start | bytes 393224 | tf_op jit(solution)/shard_map/ppermute | solution.py:16
  15.3 10.5 %collective-permute-start.8 = (bf16[8,8192]{1,0:T(8,128)(2,1)S(1)}, bf16[8,8192]{1,0:T(8,128)(2,1)S(1)}, u32[]{:S(2)}, u32[]{:S(2)}) collective-permute-start(bf16[8,8192]{1,0:T(8,128)(2,1)S(1)} %collective-permute-done.7), channel_id=1, source_target_pairs={{0,1},{1,0},{2,3},{3,2},{4,5},{5,4},{6,7},{7,6},{8,9},{9,8},{10,11... | collective-permute-start | bytes 393224 | tf_op jit(solution)/shard_map/ppermute | solution.py:16
  16.9 4.2 %collective-permute-start.9 = (bf16[8,8192]{1,0:T(8,128)(2,1)S(1)}, bf16[8,8192]{1,0:T(8,128)(2,1)S(1)}, u32[]{:S(2)}, u32[]{:S(2)}) collective-permute-start(bf16[8,8192]{1,0:T(8,128)(2,1)S(1)} %collective-permute-done.7), channel_id=1, source_target_pairs={{0,2},{1,3},{2,0},{3,1},{4,6},{5,7},{6,4},{7,5},{8,10},{9,11},{10,... | collective-permute-start | bytes 393224 | tf_op jit(solution)/shard_map/ppermute | solution.py:16
  17.1 8.7 %collective-permute-start.12 = (bf16[8,8192]{1,0:T(8,128)(2,1)S(1)}, bf16[8,8192]{1,0:T(8,128)(2,1)S(1)}, u32[]{:S(2)}, u32[]{:S(2)}) collective-permute-start(bf16[8,8192]{1,0:T(8,128)(2,1)S(1)} %collective-permute-done.11), channel_id=1, source_target_pairs={{0,1},{1,0},{2,3},{3,2},{4,5},{5,4},{6,7},{7,6},{8,9},{9,8},{10,11... | collective-permute-start | bytes 393224 | tf_op jit(solution)/shard_map/ppermute | solution.py:16
  19.4 5.6 %collective-permute-start.13 = (bf16[8,8192]{1,0:T(8,128)(2,1)S(1)}, bf16[8,8192]{1,0:T(8,128)(2,1)S(1)}, u32[]{:S(2)}, u32[]{:S(2)}) collective-permute-start(bf16[8,8192]{1,0:T(8,128)(2,1)S(1)} %collective-permute-done.11), channel_id=1, source_target_pairs={{0,2},{1,3},{2,0},{3,1},{4,6},{5,7},{6,4},{7,5},{8,10},{9,11},{10,... | collective-permute-start | bytes 393224 | tf_op jit(solution)/shard_map/ppermute | solution.py:16
  20.7 5.0 %collective-permute-start.6 = (bf16[8,8192]{1,0:T(8,128)(2,1)S(1)}, bf16[8,8192]{1,0:T(8,128)(2,1)S(1)}, u32[]{:S(2)}, u32[]{:S(2)}) collective-permute-start(bf16[8,8192]{1,0:T(8,128)(2,1)S(1)} %collective-permute-done.5), channel_id=1, source_target_pairs={{0,1},{1,0},{2,3},{3,2},{4,5},{5,4},{6,7},{7,6},{8,9},{9,8},{10,11... | collective-permute-start | bytes 393224 | tf_op jit(solution)/shard_map/ppermute | solution.py:16
  21.1 4.8 %collective-permute-start.10 = (bf16[8,8192]{1,0:T(8,128)(2,1)S(1)}, bf16[8,8192]{1,0:T(8,128)(2,1)S(1)}, u32[]{:S(2)}, u32[]{:S(2)}) collective-permute-start(bf16[8,8192]{1,0:T(8,128)(2,1)S(1)} %collective-permute-done.9), channel_id=1, source_target_pairs={{0,1},{1,0},{2,3},{3,2},{4,5},{5,4},{6,7},{7,6},{8,9},{9,8},{10,11... | collective-permute-start | bytes 393224 | tf_op jit(solution)/shard_map/ppermute | solution.py:16
  25.0 1.7 %collective-permute-start.14 = (bf16[8,8192]{1,0:T(8,128)(2,1)S(1)}, bf16[8,8192]{1,0:T(8,128)(2,1)S(1)}, u32[]{:S(2)}, u32[]{:S(2)}) collective-permute-start(bf16[8,8192]{1,0:T(8,128)(2,1)S(1)} %collective-permute-done.13), channel_id=1, source_target_pairs={{0,1},{1,0},{2,3},{3,2},{4,5},{5,4},{6,7},{7,6},{8,9},{9,8},{10,11... | collective-permute-start | bytes 393224 | tf_op jit(solution)/shard_map/ppermute | solution.py:16
  29.1 1.0 %copy-start.2 = (bf16[16,16,1792]{2,1,0:T(8,128)(2,1)}, bf16[16,16,1792]{2,1,0:T(8,128)(2,1)S(1)}, u32[]{:S(2)}) copy-start(bf16[16,16,1792]{2,1,0:T(8,128)(2,1)S(1)} %shard_map.64) | copy-start | bytes 2752516
  30.1 27.9 %all-to-all-start = ((bf16[16,16,1792]{2,1,0:T(8,128)(2,1)}), bf16[16,16,1792]{2,1,0:T(8,128)(2,1)S(1)}, u32[]{:S(2)}, u32[]{:S(2)}) async-start(bf16[16,16,1792]{2,1,0:T(8,128)(2,1)} %copy-done.2), calls=%async_computation | async-start | bytes 1835008 | tf_op jit(solution)/shard_map/all_to_all | solution.py:125
  58.0 1.2 %copy-start.1 = (f32[128,1792]{1,0:T(8,128)S(1)}, f32[128,1792]{1,0:T(8,128)}, u32[]{:S(2)}) copy-start(f32[128,1792]{1,0:T(8,128)} %fusion.5.base_ref) | copy-start | bytes 2752516

commit v2 on v1

v2 whole, which is shorter than its diff:
```python
import functools

import jax
import jax.numpy as jnp
from jax import lax
from jax.experimental import pallas as pl
from jax.experimental.pallas import tpu as pltpu
from jax.sharding import PartitionSpec as P

CAP = 16
AXIS = "adapt"
MIB = 1 << 20
STEP = 1024
PLAN_FLOPS = 6_000_000_000
VMEM = pl.BlockSpec(memory_space=pltpu.VMEM)
SMEM = pl.BlockSpec(memory_space=pltpu.SMEM)
HBM = pl.BlockSpec(memory_space=pltpu.HBM)


def swap(x, mask, count):
    return lax.ppermute(x, AXIS, [(i, i ^ mask) for i in range(count)])


def after(value, *others):
    return lax.optimization_barrier((value, *others))[0]


def gather_rows(x, count, early=()):
    far, bits = count // 2, []
    beside = swap(x, 1, count)
    chunks = {0: x, far: swap(x, far, count)}
    bit = far // 2
    while bit > 1:
        chunks[bit] = swap(x, bit, count)
        bits.append(bit)
        bit //= 2
    late = after(x, beside)
    for key in range(4, far, 4):
        chunks[far ^ key] = swap(late, far ^ key, count)
        if key not in chunks:
            chunks[key] = swap(late, key, count)
    chunks[far] = after(chunks[far], *early)
    for key in sorted(chunks):
        if key ^ 2 not in chunks:
            chunks[key ^ 2] = swap(chunks[key], 2, count)
    for key in sorted(chunks):
        chunks[key ^ 1] = swap(chunks[key], 1, count) if key else beside
    return [chunks[m] for m in range(count)]


def iota(shape, dim):
    return lax.broadcasted_iota(jnp.int32, shape, dim)


def one_hot(condition):
    return jnp.where(condition, 1.0, 0.0).astype(jnp.bfloat16)


def product(a, b):
    return jnp.dot(a, b, preferred_element_type=jnp.float32)


def ranks(ids, adapters):
    rows = ids.shape[1]
    matches = ids == iota((adapters, rows), 0)
    earlier = one_hot(iota((rows, rows), 0) < iota((rows, rows), 1))
    before = product(one_hot(matches), earlier)
    return jnp.sum(jnp.where(matches, before, 0.0), axis=0, keepdims=True).astype(jnp.int32)


def origins(me, adapters, rows):
    place = iota((1, rows), 1)
    each = rows // adapters
    return ((place // each) ^ me) * each + place % each


def picks_of(ids, me, owned, adapters):
    rows = ids.shape[1]
    pick = one_hot((ids == owned) & (ranks(ids, adapters) == iota((CAP, rows), 0)))
    back = one_hot(iota((rows, rows), 0) == origins(me, adapters, rows))
    return product(pick, back).astype(jnp.bfloat16)


def places_of(ids, adapters, slots):
    rows = ids.shape[1]
    return one_hot(ids * CAP + ranks(ids, adapters) == iota((slots, rows), 0))


def plan_kernel(count, me_ref, ids_ref, down_ref, pick_ref, turned_ref):
    pick_ref[...] = picks_of(ids_ref[...], me_ref[0], me_ref[0], count)
    turned_ref[...] = down_ref[...].T


def make_plan(ids, down, me, count):
    rows = ids.shape[1]
    return pl.pallas_call(
        functools.partial(plan_kernel, count),
        out_shape=(
            jax.ShapeDtypeStruct((CAP, rows), jnp.bfloat16),
            jax.ShapeDtypeStruct(down.shape[::-1], jnp.bfloat16),
        ),
        in_specs=[SMEM, VMEM, VMEM],
        out_specs=(VMEM, VMEM),
        compiler_params=pltpu.CompilerParams(vmem_limit_bytes=24 * MIB),
        cost_estimate=pl.CostEstimate(flops=PLAN_FLOPS, bytes_accessed=MIB, transcendentals=0),
        name="plan",
    )(me, ids, down)


def join(pairs, chunk_refs, x_ref):
    each = chunk_refs[0].shape[0]
    for i, pair in enumerate(pairs):
        both = jnp.concatenate([chunk_refs[2 * i][...], chunk_refs[2 * i + 1][...]], axis=0)
        x_ref[pair * 2 * each : (pair + 1) * 2 * each, :] = both


def late_rows(rest_hbm, x_ref, sem, inward):
    copies = []
    for i in range(sem.shape[0]):
        each = rest_hbm.shape[0] // sem.shape[0]
        outer = rest_hbm.at[pl.ds(i * each, each)]
        inner = x_ref.at[pl.ds((2 * i + 1) * each, each)]
        ends = (outer, inner) if inward else (inner, outer)
        copies.append(pltpu.make_async_copy(*ends, sem.at[i]))
        copies[-1].start()
    return copies


def delta_kernel(scale_ref, pick_ref, down_ref, up_ref, *refs):
    chunk_refs, (out_hbm, rest_hbm, x_ref, out_ref, sem, rest_sem) = refs[:-6], refs[-6:]
    count, _, width = out_ref.shape
    join(range(count // 2), chunk_refs, x_ref)
    copies = late_rows(rest_hbm, x_ref, rest_sem, False)
    low = (product(x_ref[...], down_ref[...]) * scale_ref[0]).astype(jnp.bfloat16)
    low = product(pick_ref[...], low).astype(jnp.bfloat16)
    for j in range(count):
        out_ref[j] = product(low, up_ref[:, j * width : (j + 1) * width]).astype(jnp.bfloat16)
        if j % 4 == 3:
            part = pl.ds(j - 3, 4)
            copies.append(pltpu.make_async_copy(out_ref.at[part], out_hbm.at[part], sem.at[j // 4]))
            copies[-1].start()
    for copy in copies:
        copy.wait()


def make_deltas(chunks, down, up, scale, pick):
    count = len(chunks)
    width = up.shape[1] // count
    each, depth = chunks[0].shape
    rows = count * each
    return pl.pallas_call(
        delta_kernel,
        out_shape=(
            pltpu.HBM((count, CAP, width), jnp.bfloat16),
            pltpu.HBM((rows // 2, depth), jnp.bfloat16),
        ),
        in_specs=[SMEM] + [VMEM] * (count + 3),
        out_specs=(HBM, HBM),
        scratch_shapes=[
            pltpu.VMEM((rows, depth), jnp.bfloat16),
            pltpu.VMEM((count, CAP, width), jnp.bfloat16),
            pltpu.SemaphoreType.DMA((count // 4,)),
            pltpu.SemaphoreType.DMA((count // 4,)),
        ],
        compiler_params=pltpu.CompilerParams(vmem_limit_bytes=24 * MIB),
        cost_estimate=pl.CostEstimate(
            flops=2 * depth * rows * 64,
            bytes_accessed=2 * (depth * rows + down.size + up.size),
            transcendentals=0,
        ),
        name="corrections",
    )(scale, pick, down, up, *chunks)


def base_kernel(weight_ref, rest_hbm, *refs):
    chunk_refs, (out_ref, x_ref, sem) = refs[:-3], refs[-3:]
    depth, width = weight_ref.shape
    size = min(STEP, depth)
    copies = late_rows(rest_hbm, x_ref, sem, True)
    join(range(0, len(chunk_refs), 2), chunk_refs, x_ref)
    out_ref[...] = jnp.zeros_like(out_ref)
    for copy in copies:
        copy.wait()

    def step(index, block_ref):
        columns = pl.ds(pl.multiple_of(index.index[0] * size, size), size)
        out_ref[...] += product(x_ref[:, columns], block_ref[...])

    pltpu.emit_pipeline(
        step,
        grid=(depth // size,),
        in_specs=[pl.BlockSpec((size, width), lambda k: (k, 0), pipeline_mode=pl.Buffered(3))],
        _explicit_indices=True,
    )(weight_ref)


def base_product(chunks, rest, weight):
    depth, width = weight.shape
    count = len(chunks)
    rows = count * chunks[0].shape[0]
    early = [chunk for m, chunk in enumerate(chunks) if not m & 2]
    return pl.pallas_call(
        base_kernel,
        out_shape=jax.ShapeDtypeStruct((rows, width), jnp.float32),
        in_specs=[HBM, HBM] + [VMEM] * len(early),
        out_specs=VMEM,
        scratch_shapes=[pltpu.VMEM((rows, depth), jnp.bfloat16), pltpu.SemaphoreType.DMA((count // 4,))],
        compiler_params=pltpu.CompilerParams(vmem_limit_bytes=24 * MIB),
        cost_estimate=pl.CostEstimate(
            flops=2 * rows * depth * width, bytes_accessed=2 * weight.size, transcendentals=0
        ),
        name="base",
    )(weight, rest, *early)


def combine_kernel(me_ref, ids_ref, base_ref, arrived_ref, out_ref, acc):
    rows = acc.shape[0]
    count = arrived_ref.shape[0] // CAP
    each = rows // count
    for m in range(count):
        at = pl.multiple_of((me_ref[0] ^ m) * each, each)
        acc[pl.ds(at, each), :] = base_ref[m * each : (m + 1) * each, :]
    pick = places_of(ids_ref[...], count, arrived_ref.shape[0])
    delta = lax.dot_general(
        pick, arrived_ref[...], (((0,), (0,)), ((), ())), preferred_element_type=jnp.float32
    )
    out_ref[...] = (acc[...] + delta).astype(jnp.bfloat16)


def combine(base, arrived, ids, me):
    rows, width = base.shape
    return pl.pallas_call(
        combine_kernel,
        out_shape=jax.ShapeDtypeStruct((rows, width), jnp.bfloat16),
        in_specs=[SMEM] + [VMEM] * 3,
        out_specs=VMEM,
        scratch_shapes=[pltpu.VMEM((rows, width), jnp.float32)],
        compiler_params=pltpu.CompilerParams(vmem_limit_bytes=24 * MIB),
        cost_estimate=pl.CostEstimate(
            flops=2 * rows * arrived.size, bytes_accessed=4 * base.size, transcendentals=0
        ),
        name="combine",
    )(me, ids, base, arrived)


def plain_body(chunks, up_weight, down, up, scale, ids, me):
    count = len(chunks)
    rows, width = ids.shape[1], up_weight.shape[1]
    x = jnp.concatenate(chunks, axis=0)
    low = lax.dot_general(x, down, (((1,), (1,)), ((), ())), preferred_element_type=jnp.float32)
    pick = picks_of(ids, me[0], me[0], count)
    low = product(pick, (low * scale[0]).astype(jnp.bfloat16)).astype(jnp.bfloat16)
    delta = product(low, up).astype(jnp.bfloat16).reshape(CAP, count, width)
    arrived = lax.all_to_all(delta, AXIS, split_axis=1, concat_axis=0, tiled=True)
    base = product(x, up_weight)[origins(me[0], count, rows)[0]]
    slot = (ids * CAP + ranks(ids, count))[0]
    return (base + arrived.reshape(count * CAP, width)[slot].astype(jnp.float32)).astype(jnp.bfloat16)


def body(count, tokens, up_weight, down, up, scale, row_index):
    me = lax.axis_index(AXIS).astype(jnp.int32)[None]
    ids = row_index.reshape(1, -1)
    down, up = jnp.swapaxes(down[0], 0, 1), up[0]
    if up_weight.shape[1] % 128:
        chunks = gather_rows(tokens, count)
        return plain_body(chunks, up_weight, down, up, scale, ids, me)
    pick, down = make_plan(ids, down, me, count)
    chunks = gather_rows(tokens, count, (pick,))
    delta, rest = make_deltas(chunks, down, up, scale, pick)
    arrived = lax.all_to_all(delta, AXIS, split_axis=0, concat_axis=0, tiled=True)
    base = base_product(chunks, rest, up_weight)
    return combine(base, arrived.reshape(count * CAP, -1), ids, me)


def solution(mesh):
    placed = (
        P(("groups", AXIS), None),
        P(None, AXIS),
        P(AXIS, None, None),
        P(AXIS, None, None),
        P(AXIS),
        P("groups", None),
    )
    return jax.shard_map(
        functools.partial(body, mesh.shape[AXIS]),
        mesh=mesh,
        in_specs=placed,
        out_specs=P("groups", AXIS),
        check_vma=False,
    )
```

time: 60.6 us -> 53.9 us (0.89)
  matrix products: 12.4 us -> 0 us
  Pallas kernels: 3.44 us -> 14.9 us
  local copies, waits for them, and re-layouts: 9.02 us -> 3.11 us
  waiting for transfers between devices: 13.5 us -> 17.2 us
  other arithmetic: 2.42 us -> 0 us
  starting transfers between devices: 18.6 us -> 17.8 us
    dot_general x1 -> x0, matrix products: 12.4 us -> none  [body(): base = jnp.dot(x, up_weight, preferred_element_type=jnp.float32)]
    pallas_call x2 -> x4, Pallas kernels: 3.44 us -> 14.9 us  [the longest x1 10.7 us: base_product(): pl.pallas_call(base_kernel, out_shape=jax.ShapeDtypeStruct((rows, width),...]
    ppermute x15, waiting for transfers between devices: 3.74 us -> 6.89 us  [swap(): return lax.ppermute(x, AXIS, [(i, i ^ mask) for i in range(count)])]
    gather x2 -> x0, local copies, waits for them, and re-layouts: 2.9 us -> none  [body(): ids_here, rank_here = (ids[place], rank[place])]
    unnamed x23 -> x12, local copies, waits for them, and re-layouts: 5.99 us -> 3.11 us
    reduce_sum x1 -> x0, other arithmetic: 0.82 us -> none  [body(): rank = jnp.sum(matches * running, axis=1) - 1]
    convert_element_type x1 -> x0, other arithmetic: 0.74 us -> none  [body(): (ids[:, None] == jnp.arange(adapters, dtype=jnp.int32)[None, :]).astype(j...]
    add x1 -> x0, other arithmetic: 0.66 us -> none  [body(): slot = (ids * CAP + rank)[:, None]]
  transfers between devices with their start and end apart: 16 -> 16, of which waited for: 4 -> 6; matrix products, arithmetic and copies ran while one was open for 36% -> 0% of each run, Pallas kernels for 0% -> 21%
where the time goes in v2:
time: 53.9 us; the launch traced here: 53.6 us
  starting transfers between devices  17.8 us (33%)
  waiting for transfers between devices  17.2 us (32%)
  Pallas kernels  14.9 us (28%)
  local copies, waits for them, and re-layouts  3.11 us (6%)
  between operations  0.73 us (1%)
    ppermute x15, starting transfers between devices, swap(): return lax.ppermute(x, AXIS, [(i, i ^ mask) for i in range(count)])  12.5 us
    pallas_call x1, Pallas kernels, base_product(): pl.pallas_call(base_kernel, out_shape=jax.ShapeDtypeStruct((rows, width),...  10.7 us
    all_to_all x1, waiting for transfers between devices, body(): lax.all_to_all(delta, AXIS, split_axis=0, concat_axis=0, tiled=True)  10.3 us
    ppermute x15, waiting for transfers between devices, swap(): return lax.ppermute(x, AXIS, [(i, i ^ mask) for i in range(count)])  6.89 us
    all_to_all x1, starting transfers between devices, body(): lax.all_to_all(delta, AXIS, split_axis=0, concat_axis=0, tiled=True)  5.23 us
    unnamed x12, local copies, waits for them, and re-layouts  3.11 us
    pallas_call x1, Pallas kernels, make_deltas(): pl.pallas_call(delta_kernel, out_shape=(pltpu.HBM((count, CAP, width), jn...  2.32 us
    pallas_call x1, Pallas kernels, combine(): pl.pallas_call(combine_kernel, out_shape=jax.ShapeDtypeStruct((rows, widt...  1.25 us
  transfers between devices with their start and end apart: 16, of which 6 were waited for; matrix products, arithmetic and copies ran while one was open for 0% of the time, Pallas kernels for 21%

profile of v2, /device:TPU:9, one launch (start us, length us, event | category | flops | bytes accessed | tf_op | source)
XLA Modules:
  0.0 53.6 jit_solution(17246715443313027206)
XLA Ops:
  0.0 0.7 %collective-permute-start = (bf16[8,8192]{1,0:T(8,128)(2,1)}, bf16[8,8192]{1,0:T(8,128)(2,1)S(1)}, u32[]{:S(2)}, u32[]{:S(2)}) collective-permute-start(bf16[8,8192]{1,0:T(8,128)(2,1)} %refs_0_.3), channel_id=1, source_target_pairs={{0,1},{1,0},{2,3},{3,2},{4,5},{5,4},{6,7},{7,6},{8,9},{9,8},{10,11... | collective-permute-start | bytes 393224 | tf_op jit(solution)/shard_map/ppermute | solution.py:21
  0.7 2.3 %collective-permute-start.7 = (bf16[8,8192]{1,0:T(8,128)(2,1)}, bf16[8,8192]{1,0:T(8,128)(2,1)S(1)}, u32[]{:S(2)}, u32[]{:S(2)}) collective-permute-start(bf16[8,8192]{1,0:T(8,128)(2,1)} %refs_0_.3), channel_id=1, source_target_pairs={{0,8},{1,9},{2,10},{3,11},{4,12},{5,13},{6,14},{7,15},{8,0},{9,1},... | collective-permute-start | bytes 393224 | tf_op jit(solution)/shard_map/ppermute | solution.py:21
  3.0 0.2 collective-permute-start.3
  3.2 1.2 %collective-permute-start.1 = (bf16[8,8192]{1,0:T(8,128)(2,1)}, bf16[8,8192]{1,0:T(8,128)(2,1)S(1)}, u32[]{:S(2)}, u32[]{:S(2)}) collective-permute-start(bf16[8,8192]{1,0:T(8,128)(2,1)} %refs_0_.3), channel_id=1, source_target_pairs={{0,2},{1,3},{2,0},{3,1},{4,6},{5,7},{6,4},{7,5},{8,10},{9,11},{10,... | collective-permute-start | bytes 393224 | tf_op jit(solution)/shard_map/ppermute | solution.py:21
  4.4 0.0 collective-permute-done.refs_1_
  4.4 0.2 collective-permute-start.11
  4.5 0.0 copy-start.3
  4.5 0.7 %copy-done.3 = s32[128,1]{0,1:T(1,128)S(1)} copy-done((s32[128,1]{0,1:T(1,128)S(1)}, s32[128,1]{0,1:T(1,128)}, u32[]{:S(2)}) %copy-start.3) | copy-done | bytes 536
  5.2 0.0 copy-start.5
  5.2 1.2 %copy-done.5 = bf16[1,8192,64]{1,2,0:T(8,128)(2,1)S(1)} copy-done((bf16[1,8192,64]{1,2,0:T(8,128)(2,1)S(1)}, bf16[1,8192,64]{1,2,0:T(8,128)(2,1)}, u32[]{:S(2)}) %copy-start.5) | copy-done | bytes 1048600
  6.4 0.0 copy-start
  6.4 0.0 copy-start.2
  6.4 0.6 %plan.1 = (bf16[16,128]{1,0:T(8,128)(2,1)S(1)}, bf16[8192,64]{1,0:T(8,128)(2,1)S(1)}) custom-call(s32[1]{0:T(128)} %bitcast.me_ref, s32[1,128]{1,0:T(1,128)S(1)} %bitcast.9, bf16[64,8192]{1,0:T(8,128)(2,1)S(1)} %bitcast.11), custom_call_target="tpu_custom_call" | custom-call | flops 6000000000 | bytes 1048576 | tf_op jit(solution)/shard_map/plan/pallas_call | solution.py:96
  7.1 2.8 %collective-permute-done.3.refs_4_.refs_2_ = bf16[8,8192]{1,0:T(8,128)(2,1)S(1)} collective-permute-done((bf16[8,8192]{1,0:T(8,128)(2,1)}, bf16[8,8192]{1,0:T(8,128)(2,1)S(1)}, u32[]{:S(2)}, u32[]{:S(2)}) %collective-permute-start.3) | collective-permute-done | bytes 131104 | tf_op jit(solution)/shard_map/ppermute | solution.py:21
  9.9 1.2 %collective-permute-start.5 = (bf16[8,8192]{1,0:T(8,128)(2,1)S(1)}, bf16[8,8192]{1,0:T(8,128)(2,1)S(1)}, u32[]{:S(2)}, u32[]{:S(2)}) collective-permute-start(bf16[8,8192]{1,0:T(8,128)(2,1)S(1)} %collective-permute-done.3.refs_4_.refs_2_), channel_id=1, source_target_pairs={{0,2},{1,3},{2,0},{3,1},{4,6},{5,7},{6,4},{7,5},{8,10},{9,11},{10,... | collective-permute-start | bytes 393224 | tf_op jit(solution)/shard_map/ppermute | solution.py:21
  11.1 0.0 collective-permute-done.7.refs_8_.refs_4_
  11.1 1.4 %collective-permute-start.4 = (bf16[8,8192]{1,0:T(8,128)(2,1)S(1)}, bf16[8,8192]{1,0:T(8,128)(2,1)S(1)}, u32[]{:S(2)}, u32[]{:S(2)}) collective-permute-start(bf16[8,8192]{1,0:T(8,128)(2,1)S(1)} %collective-permute-done.3.refs_4_.refs_2_), channel_id=1, source_target_pairs={{0,1},{1,0},{2,3},{3,2},{4,5},{5,4},{6,7},{7,6},{8,9},{9,8},{10,11... | collective-permute-start | bytes 393224 | tf_op jit(solution)/shard_map/ppermute | solution.py:21
  12.5 0.0 collective-permute-done.1.refs_2_
  12.5 0.1 collective-permute-start.2
  12.6 0.3 collective-permute-start.9
  12.9 2.0 %collective-permute-done.11.refs_12_.refs_6_ = bf16[8,8192]{1,0:T(8,128)(2,1)S(1)} collective-permute-done((bf16[8,8192]{1,0:T(8,128)(2,1)}, bf16[8,8192]{1,0:T(8,128)(2,1)S(1)}, u32[]{:S(2)}, u32[]{:S(2)}) %collective-permute-start.11) | collective-permute-done | bytes 131104 | tf_op jit(solution)/shard_map/ppermute | solution.py:21
  14.9 1.2 %collective-permute-start.13 = (bf16[8,8192]{1,0:T(8,128)(2,1)S(1)}, bf16[8,8192]{1,0:T(8,128)(2,1)S(1)}, u32[]{:S(2)}, u32[]{:S(2)}) collective-permute-start(bf16[8,8192]{1,0:T(8,128)(2,1)S(1)} %collective-permute-done.11.refs_12_.refs_6_), channel_id=1, source_target_pairs={{0,2},{1,3},{2,0},{3,1},{4,6},{5,7},{6,4},{7,5},{8,10},{9,11},{10,... | collective-permute-start | bytes 393224 | tf_op jit(solution)/shard_map/ppermute | solution.py:21
  16.1 0.0 collective-permute-done.5.refs_6_
  16.1 0.7 %collective-permute-start.8 = (bf16[8,8192]{1,0:T(8,128)(2,1)S(1)}, bf16[8,8192]{1,0:T(8,128)(2,1)S(1)}, u32[]{:S(2)}, u32[]{:S(2)}) collective-permute-start(bf16[8,8192]{1,0:T(8,128)(2,1)S(1)} %collective-permute-done.7.refs_8_.refs_4_), channel_id=1, source_target_pairs={{0,1},{1,0},{2,3},{3,2},{4,5},{5,4},{6,7},{7,6},{8,9},{9,8},{10,11... | collective-permute-start | bytes 393224 | tf_op jit(solution)/shard_map/ppermute | solution.py:21
  16.8 0.0 collective-permute-done.4.refs_5_.refs_3_
  16.8 0.1 collective-permute-start.12
  16.9 0.0 collective-permute-done.2.refs_3_
  16.9 0.4 collective-permute-start.6
  17.3 0.5 collective-permute-done.9.refs_10_
  17.8 1.6 %collective-permute-start.10 = (bf16[8,8192]{1,0:T(8,128)(2,1)S(1)}, bf16[8,8192]{1,0:T(8,128)(2,1)S(1)}, u32[]{:S(2)}, u32[]{:S(2)}) collective-permute-start(bf16[8,8192]{1,0:T(8,128)(2,1)S(1)} %collective-permute-done.9.refs_10_), channel_id=1, source_target_pairs={{0,1},{1,0},{2,3},{3,2},{4,5},{5,4},{6,7},{7,6},{8,9},{9,8},{10,11... | collective-permute-start | bytes 393224 | tf_op jit(solution)/shard_map/ppermute | solution.py:21
  19.4 1.2 %collective-permute-done.13.refs_14_ = bf16[8,8192]{1,0:T(8,128)(2,1)S(1)} collective-permute-done((bf16[8,8192]{1,0:T(8,128)(2,1)S(1)}, bf16[8,8192]{1,0:T(8,128)(2,1)S(1)}, u32[]{:S(2)}, u32[]{:S(2)}) %collective-permute-start.13) | collective-permute-done | bytes 131104 | tf_op jit(solution)/shard_map/ppermute | solution.py:21
  20.6 1.0 %collective-permute-start.14 = (bf16[8,8192]{1,0:T(8,128)(2,1)S(1)}, bf16[8,8192]{1,0:T(8,128)(2,1)S(1)}, u32[]{:S(2)}, u32[]{:S(2)}) collective-permute-start(bf16[8,8192]{1,0:T(8,128)(2,1)S(1)} %collective-permute-done.13.refs_14_), channel_id=1, source_target_pairs={{0,1},{1,0},{2,3},{3,2},{4,5},{5,4},{6,7},{7,6},{8,9},{9,8},{10,11... | collective-permute-start | bytes 393224 | tf_op jit(solution)/shard_map/ppermute | solution.py:21
  22.3 0.0 collective-permute-done.8.refs_9_.refs_5_
  22.3 0.0 collective-permute-done.6.refs_7_
  22.3 0.0 collective-permute-done.12.refs_13_.refs_7_
  22.3 0.0 collective-permute-done.10.refs_11_
  22.3 0.3 collective-permute-done.14.refs_15_
  22.6 0.0 copy-done
  22.6 0.0 copy-done.2
  22.6 2.3 %corrections.1 = (bf16[16,16,1792]{2,1,0:T(8,128)(2,1)}, bf16[64,8192]{1,0:T(8,128)(2,1)}) custom-call(f32[1]{0:T(128)S(6)} %copy.7.scale_ref, bf16[16,128]{1,0:T(8,128)(2,1)S(1)} %get-tuple-element.11.pick_ref, bf16[8192,64]{1,0:T(8,128)(2,1)S(1)} %get-tuple-element.12.down_ref, bf16[64,28672]{1,0:T(8,128)(2,1)S(1)} %bitcast.7, ...), custom_call_target="tpu_custom_call" | custom-call | flops 134217728 | bytes 6815744 | tf_op jit(solution)/shard_map/corrections/pallas_call | solution.py:151
  25.0 5.2 %all-to-all-start = ((bf16[16,16,1792]{2,1,0:T(8,128)(2,1)}), bf16[16,16,1792]{2,1,0:T(8,128)(2,1)S(1)}, u32[]{:S(2)}, u32[]{:S(2)}) async-start(bf16[16,16,1792]{2,1,0:T(8,128)(2,1)} %get-tuple-element.16), calls=%async_computation | async-start | bytes 1835008 | tf_op jit(solution)/shard_map/all_to_all | solution.py:270
  30.2 0.0 copy-start.1
  30.2 1.2 %copy-done.1 = bf16[64,8192]{1,0:T(8,128)(2,1)S(1)} copy-done((bf16[64,8192]{1,0:T(8,128)(2,1)S(1)}, bf16[64,8192]{1,0:T(8,128)(2,1)}, u32[]{:S(2)}) %copy-start.1) | copy-done | bytes 1048600
  31.4 0.0 copy-start.4
  31.4 10.7 %base.1.base_ref = f32[128,1792]{1,0:T(8,128)S(1)} custom-call(bf16[8192,1792]{1,0:T(8,128)(2,1)} %weight_ref.1, bf16[64,8192]{1,0:T(8,128)(2,1)S(1)} %copy-done.1, bf16[8,8192]{1,0:T(8,128)(2,1)S(1)} %copy-done.2, bf16[8,8192]{1,0:T(8,128)(2,1)S(1)} %collective-permute-done.refs_1_, bf16[8,8192]{1,0:T(8,128)(2,1)S(1)} %collective-permute-done.3.refs_4_.refs_2_, ...), custom_call_target="tpu_custom_call" | custom-call | flops 3758096384 | bytes 29360128 | tf_op jit(solution)/shard_map/base/pallas_call | solution.py:202
  42.1 10.3 %all-to-all-done = bf16[16,16,1792]{2,1,0:T(8,128)(2,1)S(1)} async-done(((bf16[16,16,1792]{2,1,0:T(8,128)(2,1)}), bf16[16,16,1792]{2,1,0:T(8,128)(2,1)S(1)}, u32[]{:S(2)}, u32[]{:S(2)}) %all-to-all-start) | async-done | bytes 917536 | tf_op jit(solution)/shard_map/all_to_all | solution.py:270
  52.4 0.0 copy-done.4
  52.4 1.3 %combine.1 = bf16[128,1792]{1,0:T(8,128)(2,1)} custom-call(s32[1]{0:T(128)} %bitcast.me_ref, s32[1,128]{1,0:T(1,128)S(1)} %bitcast.10, f32[128,1792]{1,0:T(8,128)S(1)} %base.1.base_ref, bf16[256,1792]{1,0:T(8,128)(2,1)S(1)} %bitcast.8), custom_call_target="tpu_custom_call" | custom-call | flops 117440512 | bytes 917504 | tf_op jit(solution)/shard_map/combine/pallas_call | solution.py:232
Async XLA Ops:
  0.0 4.4 %collective-permute-start = (bf16[8,8192]{1,0:T(8,128)(2,1)}, bf16[8,8192]{1,0:T(8,128)(2,1)S(1)}, u32[]{:S(2)}, u32[]{:S(2)}) collective-permute-start(bf16[8,8192]{1,0:T(8,128)(2,1)} %refs_0_.3), channel_id=1, source_target_pairs={{0,1},{1,0},{2,3},{3,2},{4,5},{5,4},{6,7},{7,6},{8,9},{9,8},{10,11... | collective-permute-start | bytes 393224 | tf_op jit(solution)/shard_map/ppermute | solution.py:21
  0.7 10.4 %collective-permute-start.7 = (bf16[8,8192]{1,0:T(8,128)(2,1)}, bf16[8,8192]{1,0:T(8,128)(2,1)S(1)}, u32[]{:S(2)}, u32[]{:S(2)}) collective-permute-start(bf16[8,8192]{1,0:T(8,128)(2,1)} %refs_0_.3), channel_id=1, source_target_pairs={{0,8},{1,9},{2,10},{3,11},{4,12},{5,13},{6,14},{7,15},{8,0},{9,1},... | collective-permute-start | bytes 393224 | tf_op jit(solution)/shard_map/ppermute | solution.py:21
  3.0 6.9 %collective-permute-start.3 = (bf16[8,8192]{1,0:T(8,128)(2,1)}, bf16[8,8192]{1,0:T(8,128)(2,1)S(1)}, u32[]{:S(2)}, u32[]{:S(2)}) collective-permute-start(bf16[8,8192]{1,0:T(8,128)(2,1)} %refs_0_.3), channel_id=1, source_target_pairs={{0,4},{1,5},{2,6},{3,7},{4,0},{5,1},{6,2},{7,3},{8,12},{9,13},{10,... | collective-permute-start | bytes 393224 | tf_op jit(solution)/shard_map/ppermute | solution.py:21
  3.2 9.4 %collective-permute-start.1 = (bf16[8,8192]{1,0:T(8,128)(2,1)}, bf16[8,8192]{1,0:T(8,128)(2,1)S(1)}, u32[]{:S(2)}, u32[]{:S(2)}) collective-permute-start(bf16[8,8192]{1,0:T(8,128)(2,1)} %refs_0_.3), channel_id=1, source_target_pairs={{0,2},{1,3},{2,0},{3,1},{4,6},{5,7},{6,4},{7,5},{8,10},{9,11},{10,... | collective-permute-start | bytes 393224 | tf_op jit(solution)/shard_map/ppermute | solution.py:21
  4.4 10.5 %collective-permute-start.11 = (bf16[8,8192]{1,0:T(8,128)(2,1)}, bf16[8,8192]{1,0:T(8,128)(2,1)S(1)}, u32[]{:S(2)}, u32[]{:S(2)}) collective-permute-start(bf16[8,8192]{1,0:T(8,128)(2,1)} %refs_0_.3), channel_id=1, source_target_pairs={{0,12},{1,13},{2,14},{3,15},{4,8},{5,9},{6,10},{7,11},{8,4},{9,5},... | collective-permute-start | bytes 393224 | tf_op jit(solution)/shard_map/ppermute | solution.py:21
  4.5 0.7 %copy-start.3 = (s32[128,1]{0,1:T(1,128)S(1)}, s32[128,1]{0,1:T(1,128)}, u32[]{:S(2)}) copy-start(s32[128,1]{0,1:T(1,128)} %param.11) | copy-start | bytes 1540
  5.2 1.2 %copy-start.5 = (bf16[1,8192,64]{1,2,0:T(8,128)(2,1)S(1)}, bf16[1,8192,64]{1,2,0:T(8,128)(2,1)}, u32[]{:S(2)}) copy-start(bf16[1,8192,64]{1,2,0:T(8,128)(2,1)} %param.8) | copy-start | bytes 3145732
  6.4 16.2 %copy-start = (bf16[1,64,28672]{2,1,0:T(8,128)(2,1)S(1)}, bf16[1,64,28672]{2,1,0:T(8,128)(2,1)}, u32[]{:S(2)}) copy-start(bf16[1,64,28672]{2,1,0:T(8,128)(2,1)} %param.9) | copy-start | bytes 11010052
  6.4 16.2 %copy-start.2 = (bf16[8,8192]{1,0:T(8,128)(2,1)S(1)}, bf16[8,8192]{1,0:T(8,128)(2,1)}, u32[]{:S(2)}) copy-start(bf16[8,8192]{1,0:T(8,128)(2,1)} %refs_0_.3) | copy-start | bytes 393220
  9.9 6.2 %collective-permute-start.5 = (bf16[8,8192]{1,0:T(8,128)(2,1)S(1)}, bf16[8,8192]{1,0:T(8,128)(2,1)S(1)}, u32[]{:S(2)}, u32[]{:S(2)}) collective-permute-start(bf16[8,8192]{1,0:T(8,128)(2,1)S(1)} %collective-permute-done.3.refs_4_.refs_2_), channel_id=1, source_target_pairs={{0,2},{1,3},{2,0},{3,1},{4,6},{5,7},{6,4},{7,5},{8,10},{9,11},{10,... | collective-permute-start | bytes 393224 | tf_op jit(solution)/shard_map/ppermute | solution.py:21
  11.1 5.7 %collective-permute-start.4 = (bf16[8,8192]{1,0:T(8,128)(2,1)S(1)}, bf16[8,8192]{1,0:T(8,128)(2,1)S(1)}, u32[]{:S(2)}, u32[]{:S(2)}) collective-permute-start(bf16[8,8192]{1,0:T(8,128)(2,1)S(1)} %collective-permute-done.3.refs_4_.refs_2_), channel_id=1, source_target_pairs={{0,1},{1,0},{2,3},{3,2},{4,5},{5,4},{6,7},{7,6},{8,9},{9,8},{10,11... | collective-permute-start | bytes 393224 | tf_op jit(solution)/shard_map/ppermute | solution.py:21
  12.5 4.4 %collective-permute-start.2 = (bf16[8,8192]{1,0:T(8,128)(2,1)S(1)}, bf16[8,8192]{1,0:T(8,128)(2,1)S(1)}, u32[]{:S(2)}, u32[]{:S(2)}) collective-permute-start(bf16[8,8192]{1,0:T(8,128)(2,1)S(1)} %collective-permute-done.1.refs_2_), channel_id=1, source_target_pairs={{0,1},{1,0},{2,3},{3,2},{4,5},{5,4},{6,7},{7,6},{8,9},{9,8},{10,11... | collective-permute-start | bytes 393224 | tf_op jit(solution)/shard_map/ppermute | solution.py:21
  12.6 5.2 %collective-permute-start.9 = (bf16[8,8192]{1,0:T(8,128)(2,1)S(1)}, bf16[8,8192]{1,0:T(8,128)(2,1)S(1)}, u32[]{:S(2)}, u32[]{:S(2)}) collective-permute-start(bf16[8,8192]{1,0:T(8,128)(2,1)S(1)} %collective-permute-done.7.refs_8_.refs_4_), channel_id=1, source_target_pairs={{0,2},{1,3},{2,0},{3,1},{4,6},{5,7},{6,4},{7,5},{8,10},{9,11},{10,... | collective-permute-start | bytes 393224 | tf_op jit(solution)/shard_map/ppermute | solution.py:21
  14.9 5.8 %collective-permute-start.13 = (bf16[8,8192]{1,0:T(8,128)(2,1)S(1)}, bf16[8,8192]{1,0:T(8,128)(2,1)S(1)}, u32[]{:S(2)}, u32[]{:S(2)}) collective-permute-start(bf16[8,8192]{1,0:T(8,128)(2,1)S(1)} %collective-permute-done.11.refs_12_.refs_6_), channel_id=1, source_target_pairs={{0,2},{1,3},{2,0},{3,1},{4,6},{5,7},{6,4},{7,5},{8,10},{9,11},{10,... | collective-permute-start | bytes 393224 | tf_op jit(solution)/shard_map/ppermute | solution.py:21
  16.1 6.2 %collective-permute-start.8 = (bf16[8,8192]{1,0:T(8,128)(2,1)S(1)}, bf16[8,8192]{1,0:T(8,128)(2,1)S(1)}, u32[]{:S(2)}, u32[]{:S(2)}) collective-permute-start(bf16[8,8192]{1,0:T(8,128)(2,1)S(1)} %collective-permute-done.7.refs_8_.refs_4_), channel_id=1, source_target_pairs={{0,1},{1,0},{2,3},{3,2},{4,5},{5,4},{6,7},{7,6},{8,9},{9,8},{10,11... | collective-permute-start | bytes 393224 | tf_op jit(solution)/shard_map/ppermute | solution.py:21
  16.8 5.5 %collective-permute-start.12 = (bf16[8,8192]{1,0:T(8,128)(2,1)S(1)}, bf16[8,8192]{1,0:T(8,128)(2,1)S(1)}, u32[]{:S(2)}, u32[]{:S(2)}) collective-permute-start(bf16[8,8192]{1,0:T(8,128)(2,1)S(1)} %collective-permute-done.11.refs_12_.refs_6_), channel_id=1, source_target_pairs={{0,1},{1,0},{2,3},{3,2},{4,5},{5,4},{6,7},{7,6},{8,9},{9,8},{10,11... | collective-permute-start | bytes 393224 | tf_op jit(solution)/shard_map/ppermute | solution.py:21
  16.9 5.4 %collective-permute-start.6 = (bf16[8,8192]{1,0:T(8,128)(2,1)S(1)}, bf16[8,8192]{1,0:T(8,128)(2,1)S(1)}, u32[]{:S(2)}, u32[]{:S(2)}) collective-permute-start(bf16[8,8192]{1,0:T(8,128)(2,1)S(1)} %collective-permute-done.5.refs_6_), channel_id=1, source_target_pairs={{0,1},{1,0},{2,3},{3,2},{4,5},{5,4},{6,7},{7,6},{8,9},{9,8},{10,11... | collective-permute-start | bytes 393224 | tf_op jit(solution)/shard_map/ppermute | solution.py:21
  17.8 4.5 %collective-permute-start.10 = (bf16[8,8192]{1,0:T(8,128)(2,1)S(1)}, bf16[8,8192]{1,0:T(8,128)(2,1)S(1)}, u32[]{:S(2)}, u32[]{:S(2)}) collective-permute-start(bf16[8,8192]{1,0:T(8,128)(2,1)S(1)} %collective-permute-done.9.refs_10_), channel_id=1, source_target_pairs={{0,1},{1,0},{2,3},{3,2},{4,5},{5,4},{6,7},{7,6},{8,9},{9,8},{10,11... | collective-permute-start | bytes 393224 | tf_op jit(solution)/shard_map/ppermute | solution.py:21
  20.6 2.0 %collective-permute-start.14 = (bf16[8,8192]{1,0:T(8,128)(2,1)S(1)}, bf16[8,8192]{1,0:T(8,128)(2,1)S(1)}, u32[]{:S(2)}, u32[]{:S(2)}) collective-permute-start(bf16[8,8192]{1,0:T(8,128)(2,1)S(1)} %collective-permute-done.13.refs_14_), channel_id=1, source_target_pairs={{0,1},{1,0},{2,3},{3,2},{4,5},{5,4},{6,7},{7,6},{8,9},{9,8},{10,11... | collective-permute-start | bytes 393224 | tf_op jit(solution)/shard_map/ppermute | solution.py:21
  25.0 27.4 %all-to-all-start = ((bf16[16,16,1792]{2,1,0:T(8,128)(2,1)}), bf16[16,16,1792]{2,1,0:T(8,128)(2,1)S(1)}, u32[]{:S(2)}, u32[]{:S(2)}) async-start(bf16[16,16,1792]{2,1,0:T(8,128)(2,1)} %get-tuple-element.16), calls=%async_computation | async-start | bytes 1835008 | tf_op jit(solution)/shard_map/all_to_all | solution.py:270
  30.2 1.2 %copy-start.1 = (bf16[64,8192]{1,0:T(8,128)(2,1)S(1)}, bf16[64,8192]{1,0:T(8,128)(2,1)}, u32[]{:S(2)}) copy-start(bf16[64,8192]{1,0:T(8,128)(2,1)} %get-tuple-element.15.rest_hbm) | copy-start | bytes 3145732
  31.4 21.0 %copy-start.4 = (s32[128,1]{0,1:T(1,128)S(1)}, s32[128,1]{0,1:T(1,128)}, u32[]{:S(2)}) copy-start(s32[128,1]{0,1:T(1,128)} %param.11) | copy-start | bytes 1540

commit v3 on v2

--- a/solution.py
+++ b/solution.py
@@ -48,6 +48,11 @@
     return [chunks[m] for m in range(count)]
 
 
+def start_order(chips):
+    near, far = list(range(1, chips // 2)), list(range(chips // 2, chips))
+    return near[:2] + far + near[2:]
+
+
 def iota(shape, dim):
     return lax.broadcasted_iota(jnp.int32, shape, dim)
 
@@ -81,9 +86,11 @@
     return product(pick, back).astype(jnp.bfloat16)
 
 
-def places_of(ids, adapters, slots):
-    rows = ids.shape[1]
-    return one_hot(ids * CAP + ranks(ids, adapters) == iota((slots, rows), 0))
+def places_of(ids, me, adapters, slots):
+    rows = ids.shape[1]
+    apart = ids ^ me
+    slot = ((apart & 1) * (adapters // 2) + apart // 2) * CAP + ranks(ids, adapters)
+    return one_hot(slot == iota((slots, rows), 0))
 
 
 def plan_kernel(count, me_ref, ids_ref, down_ref, pick_ref, turned_ref):
@@ -114,54 +121,34 @@
         x_ref[pair * 2 * each : (pair + 1) * 2 * each, :] = both
 
 
-def late_rows(rest_hbm, x_ref, sem, inward):
-    copies = []
-    for i in range(sem.shape[0]):
-        each = rest_hbm.shape[0] // sem.shape[0]
-        outer = rest_hbm.at[pl.ds(i * each, each)]
-        inner = x_ref.at[pl.ds((2 * i + 1) * each, each)]
-        ends = (outer, inner) if inward else (inner, outer)
-        copies.append(pltpu.make_async_copy(*ends, sem.at[i]))
-        copies[-1].start()
-    return copies
-
-
-def delta_kernel(scale_ref, pick_ref, down_ref, up_ref, *refs):
-    chunk_refs, (out_hbm, rest_hbm, x_ref, out_ref, sem, rest_sem) = refs[:-6], refs[-6:]
-    count, _, width = out_ref.shape
-    join(range(count // 2), chunk_refs, x_ref)
-    copies = late_rows(rest_hbm, x_ref, rest_sem, False)
+def delta_kernel(scale_ref, me_ref, pick_ref, down_ref, up_ref, *refs):
+    chips = (len(refs) - 1) // 3
+    chunk_refs, out_refs, x_ref = refs[: 2 * chips], refs[2 * chips : -1], refs[-1]
+    width = out_refs[0].shape[1]
+    join(range(chips), chunk_refs, x_ref)
     low = (product(x_ref[...], down_ref[...]) * scale_ref[0]).astype(jnp.bfloat16)
     low = product(pick_ref[...], low).astype(jnp.bfloat16)
-    for j in range(count):
-        out_ref[j] = product(low, up_ref[:, j * width : (j + 1) * width]).astype(jnp.bfloat16)
-        if j % 4 == 3:
-            part = pl.ds(j - 3, 4)
-            copies.append(pltpu.make_async_copy(out_ref.at[part], out_hbm.at[part], sem.at[j // 4]))
-            copies[-1].start()
-    for copy in copies:
-        copy.wait()
-
-
-def make_deltas(chunks, down, up, scale, pick):
+    for i, ref in enumerate(out_refs):
+        for core in range(2):
+            device = me_ref[0] ^ (2 * i + core)
+            columns = pl.ds(pl.multiple_of(device * width, 128), width)
+            delta = product(low, up_ref[:, columns])
+            ref[core * CAP : (core + 1) * CAP, :] = delta.astype(jnp.bfloat16)
+
+
+def make_deltas(chunks, down, up, scale, pick, me):
     count = len(chunks)
     width = up.shape[1] // count
     each, depth = chunks[0].shape
     rows = count * each
     return pl.pallas_call(
         delta_kernel,
-        out_shape=(
-            pltpu.HBM((count, CAP, width), jnp.bfloat16),
-            pltpu.HBM((rows // 2, depth), jnp.bfloat16),
-        ),
-        in_specs=[SMEM] + [VMEM] * (count + 3),
-        out_specs=(HBM, HBM),
-        scratch_shapes=[
-            pltpu.VMEM((rows, depth), jnp.bfloat16),
-            pltpu.VMEM((count, CAP, width), jnp.bfloat16),
-            pltpu.SemaphoreType.DMA((count // 4,)),
-            pltpu.SemaphoreType.DMA((count // 4,)),
-        ],
+        out_shape=tuple(
+            jax.ShapeDtypeStruct((2 * CAP, width), jnp.bfloat16) for _ in range(count // 2)
+        )
+        + (jax.ShapeDtypeStruct((rows, depth), jnp.bfloat16),),
+        in_specs=[SMEM, SMEM] + [VMEM] * (count + 3),
+        out_specs=(VMEM,) * (count // 2 + 1),
         compiler_params=pltpu.CompilerParams(vmem_limit_bytes=24 * MIB),
         cost_estimate=pl.CostEstimate(
             flops=2 * depth * rows * 64,
@@ -169,22 +156,20 @@
             transcendentals=0,
         ),
         name="corrections",
-    )(scale, pick, down, up, *chunks)
-
-
-def base_kernel(weight_ref, rest_hbm, *refs):
-    chunk_refs, (out_ref, x_ref, sem) = refs[:-3], refs[-3:]
+    )(scale, me, pick, down, up, *chunks)
+
+
+def base_kernel(me_ref, ids_ref, x_ref, weight_ref, out_ref, place_ref, acc):
     depth, width = weight_ref.shape
     size = min(STEP, depth)
-    copies = late_rows(rest_hbm, x_ref, sem, True)
-    join(range(0, len(chunk_refs), 2), chunk_refs, x_ref)
-    out_ref[...] = jnp.zeros_like(out_ref)
-    for copy in copies:
-        copy.wait()
+    rows, slots = place_ref.shape
+    count = slots // CAP
+    place_ref[...] = places_of(ids_ref[...], me_ref[0], count, slots).T
+    acc[...] = jnp.zeros_like(acc)
 
     def step(index, block_ref):
         columns = pl.ds(pl.multiple_of(index.index[0] * size, size), size)
-        out_ref[...] += product(x_ref[:, columns], block_ref[...])
+        acc[...] += product(x_ref[:, columns], block_ref[...])
 
     pltpu.emit_pipeline(
         step,
@@ -192,55 +177,71 @@
         in_specs=[pl.BlockSpec((size, width), lambda k: (k, 0), pipeline_mode=pl.Buffered(3))],
         _explicit_indices=True,
     )(weight_ref)
-
-
-def base_product(chunks, rest, weight):
-    depth, width = weight.shape
-    count = len(chunks)
-    rows = count * chunks[0].shape[0]
-    early = [chunk for m, chunk in enumerate(chunks) if not m & 2]
-    return pl.pallas_call(
-        base_kernel,
-        out_shape=jax.ShapeDtypeStruct((rows, width), jnp.float32),
-        in_specs=[HBM, HBM] + [VMEM] * len(early),
-        out_specs=VMEM,
-        scratch_shapes=[pltpu.VMEM((rows, depth), jnp.bfloat16), pltpu.SemaphoreType.DMA((count // 4,))],
-        compiler_params=pltpu.CompilerParams(vmem_limit_bytes=24 * MIB),
-        cost_estimate=pl.CostEstimate(
-            flops=2 * rows * depth * width, bytes_accessed=2 * weight.size, transcendentals=0
-        ),
-        name="base",
-    )(weight, rest, *early)
-
-
-def combine_kernel(me_ref, ids_ref, base_ref, arrived_ref, out_ref, acc):
-    rows = acc.shape[0]
-    count = arrived_ref.shape[0] // CAP
     each = rows // count
     for m in range(count):
         at = pl.multiple_of((me_ref[0] ^ m) * each, each)
-        acc[pl.ds(at, each), :] = base_ref[m * each : (m + 1) * each, :]
-    pick = places_of(ids_ref[...], count, arrived_ref.shape[0])
-    delta = lax.dot_general(
-        pick, arrived_ref[...], (((0,), (0,)), ((), ())), preferred_element_type=jnp.float32
-    )
-    out_ref[...] = (acc[...] + delta).astype(jnp.bfloat16)
-
-
-def combine(base, arrived, ids, me):
+        out_ref[pl.ds(at, each), :] = acc[m * each : (m + 1) * each, :]
+
+
+def base_product(x, weight, ids, me, count):
+    rows, depth = x.shape
+    width = weight.shape[1]
+    slots = count * CAP
+    return pl.pallas_call(
+        base_kernel,
+        out_shape=(
+            jax.ShapeDtypeStruct((rows, width), jnp.float32),
+            jax.ShapeDtypeStruct((rows, slots), jnp.bfloat16),
+        ),
+        in_specs=[SMEM, VMEM, VMEM, HBM],
+        out_specs=(VMEM, VMEM),
+        scratch_shapes=[pltpu.VMEM((rows, width), jnp.float32)],
+        compiler_params=pltpu.CompilerParams(vmem_limit_bytes=24 * MIB),
+        cost_estimate=pl.CostEstimate(
+            flops=2 * rows * depth * width, bytes_accessed=2 * weight.size, transcendentals=0
+        ),
+        name="base",
+    )(me, ids, x, weight)
+
+
+def combine_kernel(place_ref, base_ref, mate_ref, *refs):
+    arrived_refs, (out_hbm, out_ref, slots, sem) = refs[:-4], refs[-4:]
+    chips = len(arrived_refs)
+    width = out_ref.shape[2]
+    for i, ref in enumerate(arrived_refs):
+        slots[i * CAP : (i + 1) * CAP, :] = ref[:CAP, :]
+    half = chips * CAP
+    slots[half:, :] = mate_ref[...]
+    copies = []
+    for i in range(out_ref.shape[0]):
+        columns = pl.ds(i * width, width)
+        delta = product(place_ref[...], slots[:, columns])
+        out_ref[i] = (base_ref[:, columns] + delta).astype(jnp.bfloat16)
+        copies.append(pltpu.make_async_copy(out_ref.at[i], out_hbm.at[:, columns], sem.at[i]))
+        copies[-1].start()
+    for copy in copies:
+        copy.wait()
+
+
+def combine(base, arrived, mate, place):
     rows, width = base.shape
+    parts = 2 if width % 256 == 0 else 1
     return pl.pallas_call(
         combine_kernel,
         out_shape=jax.ShapeDtypeStruct((rows, width), jnp.bfloat16),
-        in_specs=[SMEM] + [VMEM] * 3,
-        out_specs=VMEM,
-        scratch_shapes=[pltpu.VMEM((rows, width), jnp.float32)],
+        in_specs=[VMEM] * (3 + len(arrived)),
+        out_specs=HBM,
+        scratch_shapes=[
+            pltpu.VMEM((parts, rows, width // parts), jnp.bfloat16),
+            pltpu.VMEM((place.shape[1], width), jnp.bfloat16),
+            pltpu.SemaphoreType.DMA((parts,)),
+        ],
         compiler_params=pltpu.CompilerParams(vmem_limit_bytes=24 * MIB),
         cost_estimate=pl.CostEstimate(
-            flops=2 * rows * arrived.size, bytes_accessed=4 * base.size, transcendentals=0
+            flops=2 * rows * place.size, bytes_accessed=4 * base.size, transcendentals=0
         ),
         name="combine",
-    )(me, ids, base, arrived)
+    )(place, base, mate, *arrived)
 
 
 def plain_body(chunks, up_weight, down, up, scale, ids, me):
@@ -266,10 +267,17 @@
         return plain_body(chunks, up_weight, down, up, scale, ids, me)
     pick, down = make_plan(ids, down, me, count)
     chunks = gather_rows(tokens, count, (pick,))
-    delta, rest = make_deltas(chunks, down, up, scale, pick)
-    arrived = lax.all_to_all(delta, AXIS, split_axis=0, concat_axis=0, tiled=True)
-    base = base_product(chunks, rest, up_weight)
-    return combine(base, arrived.reshape(count * CAP, -1), ids, me)
+    *deltas, x = make_deltas(chunks, down, up, scale, pick, me)
+    arrived = {0: deltas[0]}
+    order = start_order(count // 2)
+    for i in order:
+        arrived[i] = swap(deltas[i], 2 * i, count)
+    base, place = base_product(x, up_weight, ids, me, count)
+    *held, base = lax.optimization_barrier((*(arrived[i] for i in order), base))
+    arrived.update(zip(order, held))
+    arrived = [arrived[i] for i in range(count // 2)]
+    mate = swap(jnp.concatenate([part[CAP:] for part in arrived], axis=0), 1, count)
+    return combine(base, arrived, mate, place)
 
 
 def solution(mesh):

time: 53.9 us -> 52.2 us (0.968)
  starting transfers between devices: 17.8 us -> 23.3 us
  waiting for transfers between devices: 17.2 us -> 12.3 us
  local copies, waits for them, and re-layouts: 3.11 us -> 1.93 us
  Pallas kernels: 14.9 us -> 13.8 us
    ppermute x15 -> x23, starting transfers between devices: 12.5 us -> 23.3 us  [swap(): return lax.ppermute(x, AXIS, [(i, i ^ mask) for i in range(count)])]
    all_to_all x1 -> x0, waiting for transfers between devices: 10.3 us -> none  [body(): lax.all_to_all(delta, AXIS, split_axis=0, concat_axis=0, tiled=True)]
    ppermute x15 -> x23, waiting for transfers between devices: 6.89 us -> 12.3 us  [swap(): return lax.ppermute(x, AXIS, [(i, i ^ mask) for i in range(count)])]
    all_to_all x1 -> x0, starting transfers between devices: 5.23 us -> none  [body(): lax.all_to_all(delta, AXIS, split_axis=0, concat_axis=0, tiled=True)]
    unnamed x12 -> x15, local copies, waits for them, and re-layouts: 3.11 us -> 1.93 us
    pallas_call x2, Pallas kernels: 13 us -> 12.1 us  [the longest x1 10.6 us: base_product(): pl.pallas_call(base_kernel, out_shape=(jax.ShapeDtypeStruct((rows, width)...]
  transfers between devices with their start and end apart: 16 -> 23, of which waited for: 6 -> 8; matrix products, arithmetic and copies ran while one was open for 0% -> 0% of each run, Pallas kernels for 21% -> 22%
where the time goes in v3:
time: 52.2 us; the launch traced here: 52 us
  starting transfers between devices  23.3 us (45%)
  Pallas kernels  13.8 us (26%)
  waiting for transfers between devices  12.3 us (24%)
  local copies, waits for them, and re-layouts  1.93 us (4%)
  between operations  0.8 us (2%)
    ppermute x23, starting transfers between devices, swap(): return lax.ppermute(x, AXIS, [(i, i ^ mask) for i in range(count)])  23.3 us
    ppermute x23, waiting for transfers between devices, swap(): return lax.ppermute(x, AXIS, [(i, i ^ mask) for i in range(count)])  12.3 us
    pallas_call x1, Pallas kernels, base_product(): pl.pallas_call(base_kernel, out_shape=(jax.ShapeDtypeStruct((rows, width)...  10.6 us
    unnamed x15, local copies, waits for them, and re-layouts  1.93 us
    pallas_call x1, Pallas kernels, make_deltas(): pl.pallas_call(delta_kernel, out_shape=tuple((jax.ShapeDtypeStruct((2 * C...  1.47 us
  transfers between devices with their start and end apart: 23, of which 8 were waited for; matrix products, arithmetic and copies ran while one was open for 0% of the time, Pallas kernels for 22%

profile of v3, /device:TPU:9, one launch (start us, length us, event | category | flops | bytes accessed | tf_op | source)
XLA Modules:
  0.0 52.0 jit_solution(4015797242986516245)
XLA Ops:
  0.0 0.7 %collective-permute-start = (bf16[8,8192]{1,0:T(8,128)(2,1)}, bf16[8,8192]{1,0:T(8,128)(2,1)S(1)}, u32[]{:S(2)}, u32[]{:S(2)}) collective-permute-start(bf16[8,8192]{1,0:T(8,128)(2,1)} %refs_0_.1), channel_id=1, source_target_pairs={{0,1},{1,0},{2,3},{3,2},{4,5},{5,4},{6,7},{7,6},{8,9},{9,8},{10,11... | collective-permute-start | bytes 393224 | tf_op jit(solution)/shard_map/ppermute | solution.py:21
  0.7 2.3 %collective-permute-start.7 = (bf16[8,8192]{1,0:T(8,128)(2,1)}, bf16[8,8192]{1,0:T(8,128)(2,1)S(1)}, u32[]{:S(2)}, u32[]{:S(2)}) collective-permute-start(bf16[8,8192]{1,0:T(8,128)(2,1)} %refs_0_.1), channel_id=1, source_target_pairs={{0,8},{1,9},{2,10},{3,11},{4,12},{5,13},{6,14},{7,15},{8,0},{9,1},... | collective-permute-start | bytes 393224 | tf_op jit(solution)/shard_map/ppermute | solution.py:21
  3.0 0.2 collective-permute-start.3
  3.2 1.2 %collective-permute-start.1 = (bf16[8,8192]{1,0:T(8,128)(2,1)}, bf16[8,8192]{1,0:T(8,128)(2,1)S(1)}, u32[]{:S(2)}, u32[]{:S(2)}) collective-permute-start(bf16[8,8192]{1,0:T(8,128)(2,1)} %refs_0_.1), channel_id=1, source_target_pairs={{0,2},{1,3},{2,0},{3,1},{4,6},{5,7},{6,4},{7,5},{8,10},{9,11},{10,... | collective-permute-start | bytes 393224 | tf_op jit(solution)/shard_map/ppermute | solution.py:21
  4.4 0.0 collective-permute-done.refs_1_
  4.4 0.2 collective-permute-start.11
  4.5 0.7 %copy-done.2 = s32[128,1]{0,1:T(1,128)S(1)} copy-done((s32[128,1]{0,1:T(1,128)S(1)}, s32[128,1]{0,1:T(1,128)}, u32[]{:S(2)}) %copy-start.2) | copy-done | bytes 536
  5.2 1.2 %copy-done.3 = bf16[1,8192,64]{1,2,0:T(8,128)(2,1)S(1)} copy-done((bf16[1,8192,64]{1,2,0:T(8,128)(2,1)S(1)}, bf16[1,8192,64]{1,2,0:T(8,128)(2,1)}, u32[]{:S(2)}) %copy-start.3) | copy-done | bytes 1048600
  6.4 0.6 %plan.1 = (bf16[16,128]{1,0:T(8,128)(2,1)S(1)}, bf16[8192,64]{1,0:T(8,128)(2,1)S(1)}) custom-call(s32[1]{0:T(128)} %bitcast.me_ref, s32[1,128]{1,0:T(1,128)S(1)} %bitcast.7, bf16[64,8192]{1,0:T(8,128)(2,1)S(1)} %bitcast.9), custom_call_target="tpu_custom_call" | custom-call | flops 6000000000 | bytes 1048576 | tf_op jit(solution)/shard_map/plan/pallas_call | solution.py:103
  7.1 2.8 %collective-permute-done.3.refs_4_ = bf16[8,8192]{1,0:T(8,128)(2,1)S(1)} collective-permute-done((bf16[8,8192]{1,0:T(8,128)(2,1)}, bf16[8,8192]{1,0:T(8,128)(2,1)S(1)}, u32[]{:S(2)}, u32[]{:S(2)}) %collective-permute-start.3) | collective-permute-done | bytes 131104 | tf_op jit(solution)/shard_map/ppermute | solution.py:21
  9.9 1.2 %collective-permute-start.5 = (bf16[8,8192]{1,0:T(8,128)(2,1)S(1)}, bf16[8,8192]{1,0:T(8,128)(2,1)S(1)}, u32[]{:S(2)}, u32[]{:S(2)}) collective-permute-start(bf16[8,8192]{1,0:T(8,128)(2,1)S(1)} %collective-permute-done.3.refs_4_), channel_id=1, source_target_pairs={{0,2},{1,3},{2,0},{3,1},{4,6},{5,7},{6,4},{7,5},{8,10},{9,11},{10,... | collective-permute-start | bytes 393224 | tf_op jit(solution)/shard_map/ppermute | solution.py:21
  11.1 0.0 collective-permute-done.7.refs_8_
  11.1 1.4 %collective-permute-start.4 = (bf16[8,8192]{1,0:T(8,128)(2,1)S(1)}, bf16[8,8192]{1,0:T(8,128)(2,1)S(1)}, u32[]{:S(2)}, u32[]{:S(2)}) collective-permute-start(bf16[8,8192]{1,0:T(8,128)(2,1)S(1)} %collective-permute-done.3.refs_4_), channel_id=1, source_target_pairs={{0,1},{1,0},{2,3},{3,2},{4,5},{5,4},{6,7},{7,6},{8,9},{9,8},{10,11... | collective-permute-start | bytes 393224 | tf_op jit(solution)/shard_map/ppermute | solution.py:21
  12.5 0.0 collective-permute-done.1.refs_2_
  12.5 0.1 collective-permute-start.2
  12.6 0.3 collective-permute-start.9
  12.9 2.0 %collective-permute-done.11.refs_12_ = bf16[8,8192]{1,0:T(8,128)(2,1)S(1)} collective-permute-done((bf16[8,8192]{1,0:T(8,128)(2,1)}, bf16[8,8192]{1,0:T(8,128)(2,1)S(1)}, u32[]{:S(2)}, u32[]{:S(2)}) %collective-permute-start.11) | collective-permute-done | bytes 131104 | tf_op jit(solution)/shard_map/ppermute | solution.py:21
  14.9 1.2 %collective-permute-start.13 = (bf16[8,8192]{1,0:T(8,128)(2,1)S(1)}, bf16[8,8192]{1,0:T(8,128)(2,1)S(1)}, u32[]{:S(2)}, u32[]{:S(2)}) collective-permute-start(bf16[8,8192]{1,0:T(8,128)(2,1)S(1)} %collective-permute-done.11.refs_12_), channel_id=1, source_target_pairs={{0,2},{1,3},{2,0},{3,1},{4,6},{5,7},{6,4},{7,5},{8,10},{9,11},{10,... | collective-permute-start | bytes 393224 | tf_op jit(solution)/shard_map/ppermute | solution.py:21
  16.1 0.0 collective-permute-done.5.refs_6_
  16.1 0.7 %collective-permute-start.8 = (bf16[8,8192]{1,0:T(8,128)(2,1)S(1)}, bf16[8,8192]{1,0:T(8,128)(2,1)S(1)}, u32[]{:S(2)}, u32[]{:S(2)}) collective-permute-start(bf16[8,8192]{1,0:T(8,128)(2,1)S(1)} %collective-permute-done.7.refs_8_), channel_id=1, source_target_pairs={{0,1},{1,0},{2,3},{3,2},{4,5},{5,4},{6,7},{7,6},{8,9},{9,8},{10,11... | collective-permute-start | bytes 393224 | tf_op jit(solution)/shard_map/ppermute | solution.py:21
  16.8 0.0 collective-permute-done.4.refs_5_
  16.8 0.1 collective-permute-start.12
  16.9 0.0 collective-permute-done.2.refs_3_
  16.9 0.4 collective-permute-start.6
  17.3 0.5 collective-permute-done.9.refs_10_
  17.8 1.6 %collective-permute-start.10 = (bf16[8,8192]{1,0:T(8,128)(2,1)S(1)}, bf16[8,8192]{1,0:T(8,128)(2,1)S(1)}, u32[]{:S(2)}, u32[]{:S(2)}) collective-permute-start(bf16[8,8192]{1,0:T(8,128)(2,1)S(1)} %collective-permute-done.9.refs_10_), channel_id=1, source_target_pairs={{0,1},{1,0},{2,3},{3,2},{4,5},{5,4},{6,7},{7,6},{8,9},{9,8},{10,11... | collective-permute-start | bytes 393224 | tf_op jit(solution)/shard_map/ppermute | solution.py:21
  19.4 1.2 %collective-permute-done.13.refs_14_ = bf16[8,8192]{1,0:T(8,128)(2,1)S(1)} collective-permute-done((bf16[8,8192]{1,0:T(8,128)(2,1)S(1)}, bf16[8,8192]{1,0:T(8,128)(2,1)S(1)}, u32[]{:S(2)}, u32[]{:S(2)}) %collective-permute-start.13) | collective-permute-done | bytes 131104 | tf_op jit(solution)/shard_map/ppermute | solution.py:21
  20.6 1.0 %collective-permute-start.14 = (bf16[8,8192]{1,0:T(8,128)(2,1)S(1)}, bf16[8,8192]{1,0:T(8,128)(2,1)S(1)}, u32[]{:S(2)}, u32[]{:S(2)}) collective-permute-start(bf16[8,8192]{1,0:T(8,128)(2,1)S(1)} %collective-permute-done.13.refs_14_), channel_id=1, source_target_pairs={{0,1},{1,0},{2,3},{3,2},{4,5},{5,4},{6,7},{7,6},{8,9},{9,8},{10,11... | collective-permute-start | bytes 393224 | tf_op jit(solution)/shard_map/ppermute | solution.py:21
  22.3 0.0 collective-permute-done.8.refs_9_
  22.3 0.0 collective-permute-done.6.refs_7_
  22.3 0.0 collective-permute-done.12.refs_13_
  22.3 0.3 collective-permute-done.14.refs_15_
  22.6 1.5 %corrections.1 = (bf16[32,1792]{1,0:T(8,128)(2,1)S(1)}, bf16[32,1792]{1,0:T(8,128)(2,1)S(1)}, bf16[32,1792]{1,0:T(8,128)(2,1)S(1)}, bf16[32,1792]{1,0:T(8,128)(2...) custom-call(f32[1]{0:T(128)S(6)} %copy.14.scale_ref, ...), custom_call_target="tpu_custom_call" | custom-call | flops 134217728 | bytes 6815744 | tf_op jit(solution)/shard_map/corrections/pallas_call | solution.py:144
  24.1 1.3 %collective-permute-start.15 = (bf16[32,1792]{1,0:T(8,128)(2,1)S(1)}, bf16[32,1792]{1,0:T(8,128)(2,1)S(1)}, u32[]{:S(2)}, u32[]{:S(2)}) collective-permute-start(bf16[32,1792]{1,0:T(8,128)(2,1)S(1)} %get-tuple-element.34), channel_id=1, source_target_pairs={{0,2},{1,3},{2,0},{3,1},{4,6},{5,7},{6,4},{7,5},{8,10},{9,11},{10,... | collective-permute-start | bytes 344072 | tf_op jit(solution)/shard_map/ppermute | solution.py:21
  25.4 0.0 collective-permute-start.16
  25.4 2.5 %collective-permute-start.17 = (bf16[32,1792]{1,0:T(8,128)(2,1)S(1)}, bf16[32,1792]{1,0:T(8,128)(2,1)S(1)}, u32[]{:S(2)}, u32[]{:S(2)}) collective-permute-start(bf16[32,1792]{1,0:T(8,128)(2,1)S(1)} %get-tuple-element.36), channel_id=1, source_target_pairs={{0,8},{1,9},{2,10},{3,11},{4,12},{5,13},{6,14},{7,15},{8,0},{9,1},... | collective-permute-start | bytes 344072 | tf_op jit(solution)/shard_map/ppermute | solution.py:21
  27.8 1.1 %collective-permute-start.19 = (bf16[32,1792]{1,0:T(8,128)(2,1)S(1)}, bf16[32,1792]{1,0:T(8,128)(2,1)S(1)}, u32[]{:S(2)}, u32[]{:S(2)}) collective-permute-start(bf16[32,1792]{1,0:T(8,128)(2,1)S(1)} %get-tuple-element.38), channel_id=1, source_target_pairs={{0,12},{1,13},{2,14},{3,15},{4,8},{5,9},{6,10},{7,11},{8,4},{9,5},... | collective-permute-start | bytes 344072 | tf_op jit(solution)/shard_map/ppermute | solution.py:21
  29.0 0.0 collective-permute-done.15.refs_1_
  29.0 1.7 %collective-permute-start.20 = (bf16[32,1792]{1,0:T(8,128)(2,1)S(1)}, bf16[32,1792]{1,0:T(8,128)(2,1)S(1)}, u32[]{:S(2)}, u32[]{:S(2)}) collective-permute-start(bf16[32,1792]{1,0:T(8,128)(2,1)S(1)} %get-tuple-element.39), channel_id=1, source_target_pairs={{0,14},{1,15},{2,12},{3,13},{4,10},{5,11},{6,8},{7,9},{8,6},{9,7},... | collective-permute-start | bytes 344072 | tf_op jit(solution)/shard_map/ppermute | solution.py:21
  30.7 2.7 %collective-permute-start.21 = (bf16[32,1792]{1,0:T(8,128)(2,1)S(1)}, bf16[32,1792]{1,0:T(8,128)(2,1)S(1)}, u32[]{:S(2)}, u32[]{:S(2)}) collective-permute-start(bf16[32,1792]{1,0:T(8,128)(2,1)S(1)} %get-tuple-element.40), channel_id=1, source_target_pairs={{0,6},{1,7},{2,4},{3,5},{4,2},{5,3},{6,0},{7,1},{8,14},{9,15},{10,... | collective-permute-start | bytes 344072 | tf_op jit(solution)/shard_map/ppermute | solution.py:21
  33.4 10.6 %base.1 = (f32[128,1792]{1,0:T(8,128)S(1)}, bf16[128,256]{1,0:T(8,128)(2,1)S(1)}) custom-call(s32[1]{0:T(128)} %bitcast.me_ref, s32[1,128]{1,0:T(1,128)S(1)} %bitcast.8, bf16[128,8192]{1,0:T(8,128)(2,1)S(1)} %get-tuple-element.32.x_ref, bf16[8192,1792]{1,0:T(8,128)(2,1)} %weight_ref.1), custom_call_target="tpu_custom_call" | custom-call | flops 3758096384 | bytes 29360128 | tf_op jit(solution)/shard_map/base/pallas_call | solution.py:190
  44.1 0.0 collective-permute-done.18.refs_5_
  44.1 0.9 %collective-permute-done.19.refs_6_ = bf16[32,1792]{1,0:T(8,128)(2,1)S(1)} collective-permute-done((bf16[32,1792]{1,0:T(8,128)(2,1)S(1)}, bf16[32,1792]{1,0:T(8,128)(2,1)S(1)}, u32[]{:S(2)}, u32[]{:S(2)}) %collective-permute-start.19) | collective-permute-done | bytes 114720 | tf_op jit(solution)/shard_map/ppermute | solution.py:21
  45.0 3.0 %collective-permute-done.20.refs_7_ = bf16[32,1792]{1,0:T(8,128)(2,1)S(1)} collective-permute-done((bf16[32,1792]{1,0:T(8,128)(2,1)S(1)}, bf16[32,1792]{1,0:T(8,128)(2,1)S(1)}, u32[]{:S(2)}, u32[]{:S(2)}) %collective-permute-start.20) | collective-permute-done | bytes 114720 | tf_op jit(solution)/shard_map/ppermute | solution.py:21
  48.0 0.0 collective-permute-done.21.refs_3_
  48.1 1.4 %collective-permute-start.22 = (bf16[128,1792]{1,0:T(8,128)(2,1)S(1)}, bf16[128,1792]{1,0:T(8,128)(2,1)S(1)}, u32[]{:S(2)}, u32[]{:S(2)}) collective-permute-start(bf16[128,1792]{1,0:T(8,128)(2,1)S(1)} %slice_dynamic-update-slice_fusion), channel_id=1, source_target_pairs={{0,1},{1,0},{2,3},{3,2},{4,5},{5,4},{6,7},{7,6},{8,9},{9,8},{10,11... | collective-permute-start | bytes 1376264 | tf_op jit(solution)/shard_map/ppermute | solution.py:21
  49.5 1.4 %collective-permute-done.22.mate_ref = bf16[128,1792]{1,0:T(8,128)(2,1)S(1)} collective-permute-done((bf16[128,1792]{1,0:T(8,128)(2,1)S(1)}, bf16[128,1792]{1,0:T(8,128)(2,1)S(1)}, u32[]{:S(2)}, u32[]{:S(2)}) %collective-permute-start.22) | collective-permute-done | bytes 458784 | tf_op jit(solution)/shard_map/ppermute | solution.py:21
  51.0 1.0 %combine.1 = bf16[128,1792]{1,0:T(8,128)(2,1)} custom-call(bf16[128,256]{1,0:T(8,128)(2,1)S(1)} %get-tuple-element.33.place_ref, f32[128,1792]{1,0:T(8,128)S(1)} %get-tuple-element.42.base_ref, bf16[128,1792]{1,0:T(8,128)(2,1)S(1)} %collective-permute-done.22.mate_ref, bf16[32,1792]{1,0:T(8,128)(2,1)S(1)} %get-tuple-element.43.refs_0_, ...), custom_call_target="tpu_custom_call" | custom-call | flops 8388608 | bytes 917504 | tf_op jit(solution)/shard_map/combine/pallas_call | solution.py:229
  (18 shorter events, 0.1 us)
Async XLA Ops:
  0.0 4.4 %collective-permute-start = (bf16[8,8192]{1,0:T(8,128)(2,1)}, bf16[8,8192]{1,0:T(8,128)(2,1)S(1)}, u32[]{:S(2)}, u32[]{:S(2)}) collective-permute-start(bf16[8,8192]{1,0:T(8,128)(2,1)} %refs_0_.1), channel_id=1, source_target_pairs={{0,1},{1,0},{2,3},{3,2},{4,5},{5,4},{6,7},{7,6},{8,9},{9,8},{10,11... | collective-permute-start | bytes 393224 | tf_op jit(solution)/shard_map/ppermute | solution.py:21
  0.7 10.4 %collective-permute-start.7 = (bf16[8,8192]{1,0:T(8,128)(2,1)}, bf16[8,8192]{1,0:T(8,128)(2,1)S(1)}, u32[]{:S(2)}, u32[]{:S(2)}) collective-permute-start(bf16[8,8192]{1,0:T(8,128)(2,1)} %refs_0_.1), channel_id=1, source_target_pairs={{0,8},{1,9},{2,10},{3,11},{4,12},{5,13},{6,14},{7,15},{8,0},{9,1},... | collective-permute-start | bytes 393224 | tf_op jit(solution)/shard_map/ppermute | solution.py:21
  3.0 6.9 %collective-permute-start.3 = (bf16[8,8192]{1,0:T(8,128)(2,1)}, bf16[8,8192]{1,0:T(8,128)(2,1)S(1)}, u32[]{:S(2)}, u32[]{:S(2)}) collective-permute-start(bf16[8,8192]{1,0:T(8,128)(2,1)} %refs_0_.1), channel_id=1, source_target_pairs={{0,4},{1,5},{2,6},{3,7},{4,0},{5,1},{6,2},{7,3},{8,12},{9,13},{10,... | collective-permute-start | bytes 393224 | tf_op jit(solution)/shard_map/ppermute | solution.py:21
  3.2 9.4 %collective-permute-start.1 = (bf16[8,8192]{1,0:T(8,128)(2,1)}, bf16[8,8192]{1,0:T(8,128)(2,1)S(1)}, u32[]{:S(2)}, u32[]{:S(2)}) collective-permute-start(bf16[8,8192]{1,0:T(8,128)(2,1)} %refs_0_.1), channel_id=1, source_target_pairs={{0,2},{1,3},{2,0},{3,1},{4,6},{5,7},{6,4},{7,5},{8,10},{9,11},{10,... | collective-permute-start | bytes 393224 | tf_op jit(solution)/shard_map/ppermute | solution.py:21
  4.4 10.5 %collective-permute-start.11 = (bf16[8,8192]{1,0:T(8,128)(2,1)}, bf16[8,8192]{1,0:T(8,128)(2,1)S(1)}, u32[]{:S(2)}, u32[]{:S(2)}) collective-permute-start(bf16[8,8192]{1,0:T(8,128)(2,1)} %refs_0_.1), channel_id=1, source_target_pairs={{0,12},{1,13},{2,14},{3,15},{4,8},{5,9},{6,10},{7,11},{8,4},{9,5},... | collective-permute-start | bytes 393224 | tf_op jit(solution)/shard_map/ppermute | solution.py:21
  4.5 0.7 %copy-start.2 = (s32[128,1]{0,1:T(1,128)S(1)}, s32[128,1]{0,1:T(1,128)}, u32[]{:S(2)}) copy-start(s32[128,1]{0,1:T(1,128)} %param.11) | copy-start | bytes 1540
  5.2 1.2 %copy-start.3 = (bf16[1,8192,64]{1,2,0:T(8,128)(2,1)S(1)}, bf16[1,8192,64]{1,2,0:T(8,128)(2,1)}, u32[]{:S(2)}) copy-start(bf16[1,8192,64]{1,2,0:T(8,128)(2,1)} %param.8) | copy-start | bytes 3145732
  6.4 16.2 %copy-start = (bf16[1,64,28672]{2,1,0:T(8,128)(2,1)S(1)}, bf16[1,64,28672]{2,1,0:T(8,128)(2,1)}, u32[]{:S(2)}) copy-start(bf16[1,64,28672]{2,1,0:T(8,128)(2,1)} %param.9) | copy-start | bytes 11010052
  6.4 16.2 %copy-start.1 = (bf16[8,8192]{1,0:T(8,128)(2,1)S(1)}, bf16[8,8192]{1,0:T(8,128)(2,1)}, u32[]{:S(2)}) copy-start(bf16[8,8192]{1,0:T(8,128)(2,1)} %refs_0_.1) | copy-start | bytes 393220
  9.9 6.2 %collective-permute-start.5 = (bf16[8,8192]{1,0:T(8,128)(2,1)S(1)}, bf16[8,8192]{1,0:T(8,128)(2,1)S(1)}, u32[]{:S(2)}, u32[]{:S(2)}) collective-permute-start(bf16[8,8192]{1,0:T(8,128)(2,1)S(1)} %collective-permute-done.3.refs_4_), channel_id=1, source_target_pairs={{0,2},{1,3},{2,0},{3,1},{4,6},{5,7},{6,4},{7,5},{8,10},{9,11},{10,... | collective-permute-start | bytes 393224 | tf_op jit(solution)/shard_map/ppermute | solution.py:21
  11.1 5.7 %collective-permute-start.4 = (bf16[8,8192]{1,0:T(8,128)(2,1)S(1)}, bf16[8,8192]{1,0:T(8,128)(2,1)S(1)}, u32[]{:S(2)}, u32[]{:S(2)}) collective-permute-start(bf16[8,8192]{1,0:T(8,128)(2,1)S(1)} %collective-permute-done.3.refs_4_), channel_id=1, source_target_pairs={{0,1},{1,0},{2,3},{3,2},{4,5},{5,4},{6,7},{7,6},{8,9},{9,8},{10,11... | collective-permute-start | bytes 393224 | tf_op jit(solution)/shard_map/ppermute | solution.py:21
  12.5 4.4 %collective-permute-start.2 = (bf16[8,8192]{1,0:T(8,128)(2,1)S(1)}, bf16[8,8192]{1,0:T(8,128)(2,1)S(1)}, u32[]{:S(2)}, u32[]{:S(2)}) collective-permute-start(bf16[8,8192]{1,0:T(8,128)(2,1)S(1)} %collective-permute-done.1.refs_2_), channel_id=1, source_target_pairs={{0,1},{1,0},{2,3},{3,2},{4,5},{5,4},{6,7},{7,6},{8,9},{9,8},{10,11... | collective-permute-start | bytes 393224 | tf_op jit(solution)/shard_map/ppermute | solution.py:21
  12.6 5.2 %collective-permute-start.9 = (bf16[8,8192]{1,0:T(8,128)(2,1)S(1)}, bf16[8,8192]{1,0:T(8,128)(2,1)S(1)}, u32[]{:S(2)}, u32[]{:S(2)}) collective-permute-start(bf16[8,8192]{1,0:T(8,128)(2,1)S(1)} %collective-permute-done.7.refs_8_), channel_id=1, source_target_pairs={{0,2},{1,3},{2,0},{3,1},{4,6},{5,7},{6,4},{7,5},{8,10},{9,11},{10,... | collective-permute-start | bytes 393224 | tf_op jit(solution)/shard_map/ppermute | solution.py:21
  14.9 5.8 %collective-permute-start.13 = (bf16[8,8192]{1,0:T(8,128)(2,1)S(1)}, bf16[8,8192]{1,0:T(8,128)(2,1)S(1)}, u32[]{:S(2)}, u32[]{:S(2)}) collective-permute-start(bf16[8,8192]{1,0:T(8,128)(2,1)S(1)} %collective-permute-done.11.refs_12_), channel_id=1, source_target_pairs={{0,2},{1,3},{2,0},{3,1},{4,6},{5,7},{6,4},{7,5},{8,10},{9,11},{10,... | collective-permute-start | bytes 393224 | tf_op jit(solution)/shard_map/ppermute | solution.py:21
  16.1 6.2 %collective-permute-start.8 = (bf16[8,8192]{1,0:T(8,128)(2,1)S(1)}, bf16[8,8192]{1,0:T(8,128)(2,1)S(1)}, u32[]{:S(2)}, u32[]{:S(2)}) collective-permute-start(bf16[8,8192]{1,0:T(8,128)(2,1)S(1)} %collective-permute-done.7.refs_8_), channel_id=1, source_target_pairs={{0,1},{1,0},{2,3},{3,2},{4,5},{5,4},{6,7},{7,6},{8,9},{9,8},{10,11... | collective-permute-start | bytes 393224 | tf_op jit(solution)/shard_map/ppermute | solution.py:21
  16.8 5.5 %collective-permute-start.12 = (bf16[8,8192]{1,0:T(8,128)(2,1)S(1)}, bf16[8,8192]{1,0:T(8,128)(2,1)S(1)}, u32[]{:S(2)}, u32[]{:S(2)}) collective-permute-start(bf16[8,8192]{1,0:T(8,128)(2,1)S(1)} %collective-permute-done.11.refs_12_), channel_id=1, source_target_pairs={{0,1},{1,0},{2,3},{3,2},{4,5},{5,4},{6,7},{7,6},{8,9},{9,8},{10,11... | collective-permute-start | bytes 393224 | tf_op jit(solution)/shard_map/ppermute | solution.py:21
  16.9 5.4 %collective-permute-start.6 = (bf16[8,8192]{1,0:T(8,128)(2,1)S(1)}, bf16[8,8192]{1,0:T(8,128)(2,1)S(1)}, u32[]{:S(2)}, u32[]{:S(2)}) collective-permute-start(bf16[8,8192]{1,0:T(8,128)(2,1)S(1)} %collective-permute-done.5.refs_6_), channel_id=1, source_target_pairs={{0,1},{1,0},{2,3},{3,2},{4,5},{5,4},{6,7},{7,6},{8,9},{9,8},{10,11... | collective-permute-start | bytes 393224 | tf_op jit(solution)/shard_map/ppermute | solution.py:21
  17.8 4.5 %collective-permute-start.10 = (bf16[8,8192]{1,0:T(8,128)(2,1)S(1)}, bf16[8,8192]{1,0:T(8,128)(2,1)S(1)}, u32[]{:S(2)}, u32[]{:S(2)}) collective-permute-start(bf16[8,8192]{1,0:T(8,128)(2,1)S(1)} %collective-permute-done.9.refs_10_), channel_id=1, source_target_pairs={{0,1},{1,0},{2,3},{3,2},{4,5},{5,4},{6,7},{7,6},{8,9},{9,8},{10,11... | collective-permute-start | bytes 393224 | tf_op jit(solution)/shard_map/ppermute | solution.py:21
  20.6 2.0 %collective-permute-start.14 = (bf16[8,8192]{1,0:T(8,128)(2,1)S(1)}, bf16[8,8192]{1,0:T(8,128)(2,1)S(1)}, u32[]{:S(2)}, u32[]{:S(2)}) collective-permute-start(bf16[8,8192]{1,0:T(8,128)(2,1)S(1)} %collective-permute-done.13.refs_14_), channel_id=1, source_target_pairs={{0,1},{1,0},{2,3},{3,2},{4,5},{5,4},{6,7},{7,6},{8,9},{9,8},{10,11... | collective-permute-start | bytes 393224 | tf_op jit(solution)/shard_map/ppermute | solution.py:21
  24.1 4.9 %collective-permute-start.15 = (bf16[32,1792]{1,0:T(8,128)(2,1)S(1)}, bf16[32,1792]{1,0:T(8,128)(2,1)S(1)}, u32[]{:S(2)}, u32[]{:S(2)}) collective-permute-start(bf16[32,1792]{1,0:T(8,128)(2,1)S(1)} %get-tuple-element.34), channel_id=1, source_target_pairs={{0,2},{1,3},{2,0},{3,1},{4,6},{5,7},{6,4},{7,5},{8,10},{9,11},{10,... | collective-permute-start | bytes 344072 | tf_op jit(solution)/shard_map/ppermute | solution.py:21
  25.4 5.4 %collective-permute-start.16 = (bf16[32,1792]{1,0:T(8,128)(2,1)S(1)}, bf16[32,1792]{1,0:T(8,128)(2,1)S(1)}, u32[]{:S(2)}, u32[]{:S(2)}) collective-permute-start(bf16[32,1792]{1,0:T(8,128)(2,1)S(1)} %get-tuple-element.35), channel_id=1, source_target_pairs={{0,4},{1,5},{2,6},{3,7},{4,0},{5,1},{6,2},{7,3},{8,12},{9,13},{10,... | collective-permute-start | bytes 344072 | tf_op jit(solution)/shard_map/ppermute | solution.py:21
  25.4 18.7 %collective-permute-start.17 = (bf16[32,1792]{1,0:T(8,128)(2,1)S(1)}, bf16[32,1792]{1,0:T(8,128)(2,1)S(1)}, u32[]{:S(2)}, u32[]{:S(2)}) collective-permute-start(bf16[32,1792]{1,0:T(8,128)(2,1)S(1)} %get-tuple-element.36), channel_id=1, source_target_pairs={{0,8},{1,9},{2,10},{3,11},{4,12},{5,13},{6,14},{7,15},{8,0},{9,1},... | collective-permute-start | bytes 344072 | tf_op jit(solution)/shard_map/ppermute | solution.py:21
  27.8 16.3 %collective-permute-start.18 = (bf16[32,1792]{1,0:T(8,128)(2,1)S(1)}, bf16[32,1792]{1,0:T(8,128)(2,1)S(1)}, u32[]{:S(2)}, u32[]{:S(2)}) collective-permute-start(bf16[32,1792]{1,0:T(8,128)(2,1)S(1)} %get-tuple-element.37), channel_id=1, source_target_pairs={{0,10},{1,11},{2,8},{3,9},{4,14},{5,15},{6,12},{7,13},{8,2},{9,3},... | collective-permute-start | bytes 344072 | tf_op jit(solution)/shard_map/ppermute | solution.py:21
  27.8 17.1 %collective-permute-start.19 = (bf16[32,1792]{1,0:T(8,128)(2,1)S(1)}, bf16[32,1792]{1,0:T(8,128)(2,1)S(1)}, u32[]{:S(2)}, u32[]{:S(2)}) collective-permute-start(bf16[32,1792]{1,0:T(8,128)(2,1)S(1)} %get-tuple-element.38), channel_id=1, source_target_pairs={{0,12},{1,13},{2,14},{3,15},{4,8},{5,9},{6,10},{7,11},{8,4},{9,5},... | collective-permute-start | bytes 344072 | tf_op jit(solution)/shard_map/ppermute | solution.py:21
  29.0 19.0 %collective-permute-start.20 = (bf16[32,1792]{1,0:T(8,128)(2,1)S(1)}, bf16[32,1792]{1,0:T(8,128)(2,1)S(1)}, u32[]{:S(2)}, u32[]{:S(2)}) collective-permute-start(bf16[32,1792]{1,0:T(8,128)(2,1)S(1)} %get-tuple-element.39), channel_id=1, source_target_pairs={{0,14},{1,15},{2,12},{3,13},{4,10},{5,11},{6,8},{7,9},{8,6},{9,7},... | collective-permute-start | bytes 344072 | tf_op jit(solution)/shard_map/ppermute | solution.py:21
  30.7 17.3 %collective-permute-start.21 = (bf16[32,1792]{1,0:T(8,128)(2,1)S(1)}, bf16[32,1792]{1,0:T(8,128)(2,1)S(1)}, u32[]{:S(2)}, u32[]{:S(2)}) collective-permute-start(bf16[32,1792]{1,0:T(8,128)(2,1)S(1)} %get-tuple-element.40), channel_id=1, source_target_pairs={{0,6},{1,7},{2,4},{3,5},{4,2},{5,3},{6,0},{7,1},{8,14},{9,15},{10,... | collective-permute-start | bytes 344072 | tf_op jit(solution)/shard_map/ppermute | solution.py:21
  48.1 2.9 %collective-permute-start.22 = (bf16[128,1792]{1,0:T(8,128)(2,1)S(1)}, bf16[128,1792]{1,0:T(8,128)(2,1)S(1)}, u32[]{:S(2)}, u32[]{:S(2)}) collective-permute-start(bf16[128,1792]{1,0:T(8,128)(2,1)S(1)} %slice_dynamic-update-slice_fusion), channel_id=1, source_target_pairs={{0,1},{1,0},{2,3},{3,2},{4,5},{5,4},{6,7},{7,6},{8,9},{9,8},{10,11... | collective-permute-start | bytes 1376264 | tf_op jit(solution)/shard_map/ppermute | solution.py:21

commit v4 on v3

--- a/solution.py
+++ b/solution.py
@@ -121,42 +121,65 @@
         x_ref[pair * 2 * each : (pair + 1) * 2 * each, :] = both
 
 
-def delta_kernel(scale_ref, me_ref, pick_ref, down_ref, up_ref, *refs):
-    chips = (len(refs) - 1) // 3
-    chunk_refs, out_refs, x_ref = refs[: 2 * chips], refs[2 * chips : -1], refs[-1]
-    width = out_refs[0].shape[1]
-    join(range(chips), chunk_refs, x_ref)
+def write_deltas(low, up_ref, first_device, ref):
+    width = ref.shape[1]
+    for core in range(2):
+        columns = pl.ds(pl.multiple_of((first_device ^ core) * width, 128), width)
+        delta = product(low, up_ref[:, columns])
+        ref[core * CAP : (core + 1) * CAP, :] = delta.astype(jnp.bfloat16)
+
+
+def low_kernel(scale_ref, me_ref, pick_ref, down_ref, up_ref, *refs):
+    chunk_refs, (out_ref, low_ref, x_ref) = refs[:-3], refs[-3:]
+    count = len(chunk_refs)
+    join(range(count // 2), chunk_refs, x_ref)
     low = (product(x_ref[...], down_ref[...]) * scale_ref[0]).astype(jnp.bfloat16)
     low = product(pick_ref[...], low).astype(jnp.bfloat16)
-    for i, ref in enumerate(out_refs):
-        for core in range(2):
-            device = me_ref[0] ^ (2 * i + core)
-            columns = pl.ds(pl.multiple_of(device * width, 128), width)
-            delta = product(low, up_ref[:, columns])
-            ref[core * CAP : (core + 1) * CAP, :] = delta.astype(jnp.bfloat16)
-
-
-def make_deltas(chunks, down, up, scale, pick, me):
+    low_ref[...] = low
+    write_deltas(low, up_ref, me_ref[0] ^ (count // 2), out_ref)
+
+
+def make_low(chunks, down, up, scale, pick, me):
     count = len(chunks)
     width = up.shape[1] // count
     each, depth = chunks[0].shape
     rows = count * each
     return pl.pallas_call(
-        delta_kernel,
-        out_shape=tuple(
-            jax.ShapeDtypeStruct((2 * CAP, width), jnp.bfloat16) for _ in range(count // 2)
-        )
-        + (jax.ShapeDtypeStruct((rows, depth), jnp.bfloat16),),
+        low_kernel,
+        out_shape=(
+            jax.ShapeDtypeStruct((2 * CAP, width), jnp.bfloat16),
+            jax.ShapeDtypeStruct((CAP, up.shape[0]), jnp.bfloat16),
+            jax.ShapeDtypeStruct((rows, depth), jnp.bfloat16),
+        ),
         in_specs=[SMEM, SMEM] + [VMEM] * (count + 3),
-        out_specs=(VMEM,) * (count // 2 + 1),
+        out_specs=(VMEM,) * 3,
         compiler_params=pltpu.CompilerParams(vmem_limit_bytes=24 * MIB),
         cost_estimate=pl.CostEstimate(
             flops=2 * depth * rows * 64,
             bytes_accessed=2 * (depth * rows + down.size + up.size),
             transcendentals=0,
         ),
+        name="low",
+    )(scale, me, pick, down, up, *chunks)
+
+
+def delta_kernel(chips, me_ref, low_ref, up_ref, *out_refs):
+    for i, ref in zip(chips, out_refs):
+        write_deltas(low_ref[...], up_ref, me_ref[0] ^ (2 * i), ref)
+
+
+def make_deltas(low, up, me, chips, width):
+    return pl.pallas_call(
+        functools.partial(delta_kernel, chips),
+        out_shape=tuple(jax.ShapeDtypeStruct((2 * CAP, width), jnp.bfloat16) for _ in chips),
+        in_specs=[SMEM, VMEM, VMEM],
+        out_specs=(VMEM,) * len(chips),
+        compiler_params=pltpu.CompilerParams(vmem_limit_bytes=24 * MIB),
+        cost_estimate=pl.CostEstimate(
+            flops=2 * 16 * up.size, bytes_accessed=2 * up.size, transcendentals=0
+        ),
         name="corrections",
-    )(scale, me, pick, down, up, *chunks)
+    )(me, low, up)
 
 
 def base_kernel(me_ref, ids_ref, x_ref, weight_ref, out_ref, place_ref, acc):
@@ -267,10 +290,15 @@
         return plain_body(chunks, up_weight, down, up, scale, ids, me)
     pick, down = make_plan(ids, down, me, count)
     chunks = gather_rows(tokens, count, (pick,))
-    *deltas, x = make_deltas(chunks, down, up, scale, pick, me)
-    arrived = {0: deltas[0]}
+    across = count // 4
+    arrived = {}
+    out, low, x = make_low(chunks, down, up, scale, pick, me)
+    arrived[across] = swap(out, 2 * across, count)
     order = start_order(count // 2)
-    for i in order:
+    others = [0] + [i for i in order if i != across]
+    deltas = dict(zip(others, make_deltas(low, up, me, others, up_weight.shape[1])))
+    arrived[0] = deltas[0]
+    for i in others[1:]:
         arrived[i] = swap(deltas[i], 2 * i, count)
     base, place = base_product(x, up_weight, ids, me, count)
     *held, base = lax.optimization_barrier((*(arrived[i] for i in order), base))

time: 52.2 us -> 50.2 us (0.962)
  waiting for transfers between devices: 12.3 us -> 10.4 us
    ppermute x23, waiting for transfers between devices: 12.3 us -> 10.4 us  [swap(): return lax.ppermute(x, AXIS, [(i, i ^ mask) for i in range(count)])]
    pallas_call x1 -> x2, Pallas kernels: 1.47 us -> 1.55 us  [the longest x1 1.02 us: make_low(): pl.pallas_call(low_kernel, out_shape=(jax.ShapeDtypeStruct((2 * CAP, widt...]
  transfers between devices with their start and end apart: 23 -> 23, of which waited for: 8 -> 7; matrix products, arithmetic and copies ran while one was open for 0% -> 0% of each run, Pallas kernels for 22% -> 24%
where the time goes in v4:
time: 50.2 us; the launch traced here: 49.9 us
  starting transfers between devices  23 us (46%)
  Pallas kernels  13.9 us (28%)
  waiting for transfers between devices  10.4 us (21%)
  local copies, waits for them, and re-layouts  1.93 us (4%)
  between operations  0.81 us (2%)
    ppermute x23, starting transfers between devices, swap(): return lax.ppermute(x, AXIS, [(i, i ^ mask) for i in range(count)])  23 us
    pallas_call x1, Pallas kernels, base_product(): pl.pallas_call(base_kernel, out_shape=(jax.ShapeDtypeStruct((rows, width)...  10.6 us
    ppermute x23, waiting for transfers between devices, swap(): return lax.ppermute(x, AXIS, [(i, i ^ mask) for i in range(count)])  10.4 us
    unnamed x15, local copies, waits for them, and re-layouts  1.93 us
    pallas_call x1, Pallas kernels, combine(): pl.pallas_call(combine_kernel, out_shape=jax.ShapeDtypeStruct((rows, widt...  1.03 us
    pallas_call x1, Pallas kernels, make_low(): pl.pallas_call(low_kernel, out_shape=(jax.ShapeDtypeStruct((2 * CAP, widt...  1.02 us
  transfers between devices with their start and end apart: 23, of which 7 were waited for; matrix products, arithmetic and copies ran while one was open for 0% of the time, Pallas kernels for 24%

profile of v4, /device:TPU:9, one launch (start us, length us, event | category | flops | bytes accessed | tf_op | source)
XLA Modules:
  0.0 49.9 jit_solution(4337225020481266414)
XLA Ops:
  0.0 0.7 %collective-permute-start = (bf16[8,8192]{1,0:T(8,128)(2,1)}, bf16[8,8192]{1,0:T(8,128)(2,1)S(1)}, u32[]{:S(2)}, u32[]{:S(2)}) collective-permute-start(bf16[8,8192]{1,0:T(8,128)(2,1)} %refs_0_.1), channel_id=1, source_target_pairs={{0,1},{1,0},{2,3},{3,2},{4,5},{5,4},{6,7},{7,6},{8,9},{9,8},{10,11... | collective-permute-start | bytes 393224 | tf_op jit(solution)/shard_map/ppermute | solution.py:21
  0.7 2.3 %collective-permute-start.7 = (bf16[8,8192]{1,0:T(8,128)(2,1)}, bf16[8,8192]{1,0:T(8,128)(2,1)S(1)}, u32[]{:S(2)}, u32[]{:S(2)}) collective-permute-start(bf16[8,8192]{1,0:T(8,128)(2,1)} %refs_0_.1), channel_id=1, source_target_pairs={{0,8},{1,9},{2,10},{3,11},{4,12},{5,13},{6,14},{7,15},{8,0},{9,1},... | collective-permute-start | bytes 393224 | tf_op jit(solution)/shard_map/ppermute | solution.py:21
  3.0 0.2 collective-permute-start.3
  3.2 1.2 %collective-permute-start.1 = (bf16[8,8192]{1,0:T(8,128)(2,1)}, bf16[8,8192]{1,0:T(8,128)(2,1)S(1)}, u32[]{:S(2)}, u32[]{:S(2)}) collective-permute-start(bf16[8,8192]{1,0:T(8,128)(2,1)} %refs_0_.1), channel_id=1, source_target_pairs={{0,2},{1,3},{2,0},{3,1},{4,6},{5,7},{6,4},{7,5},{8,10},{9,11},{10,... | collective-permute-start | bytes 393224 | tf_op jit(solution)/shard_map/ppermute | solution.py:21
  4.4 0.0 collective-permute-done.refs_1_
  4.4 0.2 collective-permute-start.11
  4.5 0.7 %copy-done.2 = s32[128,1]{0,1:T(1,128)S(1)} copy-done((s32[128,1]{0,1:T(1,128)S(1)}, s32[128,1]{0,1:T(1,128)}, u32[]{:S(2)}) %copy-start.2) | copy-done | bytes 536
  5.2 1.2 %copy-done.3 = bf16[1,8192,64]{1,2,0:T(8,128)(2,1)S(1)} copy-done((bf16[1,8192,64]{1,2,0:T(8,128)(2,1)S(1)}, bf16[1,8192,64]{1,2,0:T(8,128)(2,1)}, u32[]{:S(2)}) %copy-start.3) | copy-done | bytes 1048600
  6.4 0.6 %plan.1 = (bf16[16,128]{1,0:T(8,128)(2,1)S(1)}, bf16[8192,64]{1,0:T(8,128)(2,1)S(1)}) custom-call(s32[1]{0:T(128)} %bitcast.me_ref, s32[1,128]{1,0:T(1,128)S(1)} %bitcast.8, bf16[64,8192]{1,0:T(8,128)(2,1)S(1)} %bitcast.10), custom_call_target="tpu_custom_call" | custom-call | flops 6000000000 | bytes 1048576 | tf_op jit(solution)/shard_map/plan/pallas_call | solution.py:103
  7.1 2.8 %collective-permute-done.3.refs_4_ = bf16[8,8192]{1,0:T(8,128)(2,1)S(1)} collective-permute-done((bf16[8,8192]{1,0:T(8,128)(2,1)}, bf16[8,8192]{1,0:T(8,128)(2,1)S(1)}, u32[]{:S(2)}, u32[]{:S(2)}) %collective-permute-start.3) | collective-permute-done | bytes 131104 | tf_op jit(solution)/shard_map/ppermute | solution.py:21
  9.9 1.2 %collective-permute-start.5 = (bf16[8,8192]{1,0:T(8,128)(2,1)S(1)}, bf16[8,8192]{1,0:T(8,128)(2,1)S(1)}, u32[]{:S(2)}, u32[]{:S(2)}) collective-permute-start(bf16[8,8192]{1,0:T(8,128)(2,1)S(1)} %collective-permute-done.3.refs_4_), channel_id=1, source_target_pairs={{0,2},{1,3},{2,0},{3,1},{4,6},{5,7},{6,4},{7,5},{8,10},{9,11},{10,... | collective-permute-start | bytes 393224 | tf_op jit(solution)/shard_map/ppermute | solution.py:21
  11.1 0.0 collective-permute-done.7.refs_8_
  11.1 1.4 %collective-permute-start.4 = (bf16[8,8192]{1,0:T(8,128)(2,1)S(1)}, bf16[8,8192]{1,0:T(8,128)(2,1)S(1)}, u32[]{:S(2)}, u32[]{:S(2)}) collective-permute-start(bf16[8,8192]{1,0:T(8,128)(2,1)S(1)} %collective-permute-done.3.refs_4_), channel_id=1, source_target_pairs={{0,1},{1,0},{2,3},{3,2},{4,5},{5,4},{6,7},{7,6},{8,9},{9,8},{10,11... | collective-permute-start | bytes 393224 | tf_op jit(solution)/shard_map/ppermute | solution.py:21
  12.5 0.0 collective-permute-done.1.refs_2_
  12.5 0.1 collective-permute-start.2
  12.6 0.3 collective-permute-start.9
  12.9 2.0 %collective-permute-done.11.refs_12_ = bf16[8,8192]{1,0:T(8,128)(2,1)S(1)} collective-permute-done((bf16[8,8192]{1,0:T(8,128)(2,1)}, bf16[8,8192]{1,0:T(8,128)(2,1)S(1)}, u32[]{:S(2)}, u32[]{:S(2)}) %collective-permute-start.11) | collective-permute-done | bytes 131104 | tf_op jit(solution)/shard_map/ppermute | solution.py:21
  14.9 1.2 %collective-permute-start.13 = (bf16[8,8192]{1,0:T(8,128)(2,1)S(1)}, bf16[8,8192]{1,0:T(8,128)(2,1)S(1)}, u32[]{:S(2)}, u32[]{:S(2)}) collective-permute-start(bf16[8,8192]{1,0:T(8,128)(2,1)S(1)} %collective-permute-done.11.refs_12_), channel_id=1, source_target_pairs={{0,2},{1,3},{2,0},{3,1},{4,6},{5,7},{6,4},{7,5},{8,10},{9,11},{10,... | collective-permute-start | bytes 393224 | tf_op jit(solution)/shard_map/ppermute | solution.py:21
  16.1 0.0 collective-permute-done.5.refs_6_
  16.1 0.7 %collective-permute-start.8 = (bf16[8,8192]{1,0:T(8,128)(2,1)S(1)}, bf16[8,8192]{1,0:T(8,128)(2,1)S(1)}, u32[]{:S(2)}, u32[]{:S(2)}) collective-permute-start(bf16[8,8192]{1,0:T(8,128)(2,1)S(1)} %collective-permute-done.7.refs_8_), channel_id=1, source_target_pairs={{0,1},{1,0},{2,3},{3,2},{4,5},{5,4},{6,7},{7,6},{8,9},{9,8},{10,11... | collective-permute-start | bytes 393224 | tf_op jit(solution)/shard_map/ppermute | solution.py:21
  16.8 0.1 collective-permute-start.12
  16.9 0.4 collective-permute-start.6
  17.3 0.5 collective-permute-done.9.refs_10_
  17.8 1.6 %collective-permute-start.10 = (bf16[8,8192]{1,0:T(8,128)(2,1)S(1)}, bf16[8,8192]{1,0:T(8,128)(2,1)S(1)}, u32[]{:S(2)}, u32[]{:S(2)}) collective-permute-start(bf16[8,8192]{1,0:T(8,128)(2,1)S(1)} %collective-permute-done.9.refs_10_), channel_id=1, source_target_pairs={{0,1},{1,0},{2,3},{3,2},{4,5},{5,4},{6,7},{7,6},{8,9},{9,8},{10,11... | collective-permute-start | bytes 393224 | tf_op jit(solution)/shard_map/ppermute | solution.py:21
  19.4 1.2 %collective-permute-done.13.refs_14_ = bf16[8,8192]{1,0:T(8,128)(2,1)S(1)} collective-permute-done((bf16[8,8192]{1,0:T(8,128)(2,1)S(1)}, bf16[8,8192]{1,0:T(8,128)(2,1)S(1)}, u32[]{:S(2)}, u32[]{:S(2)}) %collective-permute-start.13) | collective-permute-done | bytes 131104 | tf_op jit(solution)/shard_map/ppermute | solution.py:21
  20.6 1.0 %collective-permute-start.14 = (bf16[8,8192]{1,0:T(8,128)(2,1)S(1)}, bf16[8,8192]{1,0:T(8,128)(2,1)S(1)}, u32[]{:S(2)}, u32[]{:S(2)}) collective-permute-start(bf16[8,8192]{1,0:T(8,128)(2,1)S(1)} %collective-permute-done.13.refs_14_), channel_id=1, source_target_pairs={{0,1},{1,0},{2,3},{3,2},{4,5},{5,4},{6,7},{7,6},{8,9},{9,8},{10,11... | collective-permute-start | bytes 393224 | tf_op jit(solution)/shard_map/ppermute | solution.py:21
  22.3 0.0 collective-permute-done.8.refs_9_
  22.3 0.0 collective-permute-done.12.refs_13_
  22.3 0.0 collective-permute-done.10.refs_11_
  22.3 0.3 collective-permute-done.14.refs_15_
  22.6 1.0 %low.1 = (bf16[32,1792]{1,0:T(8,128)(2,1)S(1)}, bf16[16,64]{1,0:T(8,128)(2,1)S(1)}, bf16[128,8192]{1,0:T(8,128)(2,1)S(1)}) custom-call(f32[1]{0:T(128)S(6)} %copy.14.scale_ref, s32[1]{0:T(128)} %bitcast.me_ref, bf16[16,128]{1,0:T(8,128)(2,1)S(1)} %get-tuple-element.29.pick_ref, bf16[8192,64]{1,0:T(8,128)(2,1)S(1)} %get-tuple-element.30.down_ref, ...), custom_call_target="tpu_custom_call" | custom-call | flops 134217728 | bytes 6815744 | tf_op jit(solution)/shard_map/low/pallas_call | solution.py:147
  23.7 0.5 collective-permute-start.17
  24.1 0.5 %corrections.1 = (bf16[32,1792]{1,0:T(8,128)(2,1)S(1)}, bf16[32,1792]{1,0:T(8,128)(2,1)S(1)}, bf16[32,1792]{1,0:T(8,128)(2,1)S(1)}, bf16[32,1792]{1,0:T(8,128)(2...) custom-call(s32[1]{0:T(128)} %bitcast.me_ref, ...), custom_call_target="tpu_custom_call" | custom-call | flops 58720256 | bytes 3670016 | tf_op jit(solution)/shard_map/corrections/pallas_call | solution.py:172
  24.7 1.1 %collective-permute-start.15 = (bf16[32,1792]{1,0:T(8,128)(2,1)S(1)}, bf16[32,1792]{1,0:T(8,128)(2,1)S(1)}, u32[]{:S(2)}, u32[]{:S(2)}) collective-permute-start(bf16[32,1792]{1,0:T(8,128)(2,1)S(1)} %get-tuple-element.36), channel_id=1, source_target_pairs={{0,2},{1,3},{2,0},{3,1},{4,6},{5,7},{6,4},{7,5},{8,10},{9,11},{10,... | collective-permute-start | bytes 344072 | tf_op jit(solution)/shard_map/ppermute | solution.py:21
  25.8 2.2 %collective-permute-start.16 = (bf16[32,1792]{1,0:T(8,128)(2,1)S(1)}, bf16[32,1792]{1,0:T(8,128)(2,1)S(1)}, u32[]{:S(2)}, u32[]{:S(2)}) collective-permute-start(bf16[32,1792]{1,0:T(8,128)(2,1)S(1)} %get-tuple-element.37), channel_id=1, source_target_pairs={{0,4},{1,5},{2,6},{3,7},{4,0},{5,1},{6,2},{7,3},{8,12},{9,13},{10,... | collective-permute-start | bytes 344072 | tf_op jit(solution)/shard_map/ppermute | solution.py:21
  28.0 1.2 %collective-permute-start.19 = (bf16[32,1792]{1,0:T(8,128)(2,1)S(1)}, bf16[32,1792]{1,0:T(8,128)(2,1)S(1)}, u32[]{:S(2)}, u32[]{:S(2)}) collective-permute-start(bf16[32,1792]{1,0:T(8,128)(2,1)S(1)} %get-tuple-element.40), channel_id=1, source_target_pairs={{0,12},{1,13},{2,14},{3,15},{4,8},{5,9},{6,10},{7,11},{8,4},{9,5},... | collective-permute-start | bytes 344072 | tf_op jit(solution)/shard_map/ppermute | solution.py:21
  29.1 0.0 collective-permute-done.17.refs_4_
  29.2 2.1 %collective-permute-start.20 = (bf16[32,1792]{1,0:T(8,128)(2,1)S(1)}, bf16[32,1792]{1,0:T(8,128)(2,1)S(1)}, u32[]{:S(2)}, u32[]{:S(2)}) collective-permute-start(bf16[32,1792]{1,0:T(8,128)(2,1)S(1)} %get-tuple-element.41), channel_id=1, source_target_pairs={{0,14},{1,15},{2,12},{3,13},{4,10},{5,11},{6,8},{7,9},{8,6},{9,7},... | collective-permute-start | bytes 344072 | tf_op jit(solution)/shard_map/ppermute | solution.py:21
  31.2 0.0 collective-permute-done.15.refs_1_
  31.2 2.4 %collective-permute-start.21 = (bf16[32,1792]{1,0:T(8,128)(2,1)S(1)}, bf16[32,1792]{1,0:T(8,128)(2,1)S(1)}, u32[]{:S(2)}, u32[]{:S(2)}) collective-permute-start(bf16[32,1792]{1,0:T(8,128)(2,1)S(1)} %get-tuple-element.42), channel_id=1, source_target_pairs={{0,6},{1,7},{2,4},{3,5},{4,2},{5,3},{6,0},{7,1},{8,14},{9,15},{10,... | collective-permute-start | bytes 344072 | tf_op jit(solution)/shard_map/ppermute | solution.py:21
  33.6 10.6 %base.1 = (f32[128,1792]{1,0:T(8,128)S(1)}, bf16[128,256]{1,0:T(8,128)(2,1)S(1)}) custom-call(s32[1]{0:T(128)} %bitcast.me_ref, s32[1,128]{1,0:T(1,128)S(1)} %bitcast.9, bf16[128,8192]{1,0:T(8,128)(2,1)S(1)} %get-tuple-element.33.x_ref, bf16[8192,1792]{1,0:T(8,128)(2,1)} %weight_ref.1), custom_call_target="tpu_custom_call" | custom-call | flops 3758096384 | bytes 29360128 | tf_op jit(solution)/shard_map/base/pallas_call | solution.py:213
  44.2 0.0 collective-permute-done.18.refs_5_
  44.3 0.0 collective-permute-done.19.refs_6_
  44.3 2.0 %collective-permute-done.20.refs_7_ = bf16[32,1792]{1,0:T(8,128)(2,1)S(1)} collective-permute-done((bf16[32,1792]{1,0:T(8,128)(2,1)S(1)}, bf16[32,1792]{1,0:T(8,128)(2,1)S(1)}, u32[]{:S(2)}, u32[]{:S(2)}) %collective-permute-start.20) | collective-permute-done | bytes 114720 | tf_op jit(solution)/shard_map/ppermute | solution.py:21
  46.3 0.0 collective-permute-done.21.refs_3_
  46.4 1.1 %collective-permute-start.22 = (bf16[128,1792]{1,0:T(8,128)(2,1)S(1)}, bf16[128,1792]{1,0:T(8,128)(2,1)S(1)}, u32[]{:S(2)}, u32[]{:S(2)}) collective-permute-start(bf16[128,1792]{1,0:T(8,128)(2,1)S(1)} %slice_dynamic-update-slice_fusion), channel_id=1, source_target_pairs={{0,1},{1,0},{2,3},{3,2},{4,5},{5,4},{6,7},{7,6},{8,9},{9,8},{10,11... | collective-permute-start | bytes 1376264 | tf_op jit(solution)/shard_map/ppermute | solution.py:21
  47.5 1.4 %collective-permute-done.22.mate_ref = bf16[128,1792]{1,0:T(8,128)(2,1)S(1)} collective-permute-done((bf16[128,1792]{1,0:T(8,128)(2,1)S(1)}, bf16[128,1792]{1,0:T(8,128)(2,1)S(1)}, u32[]{:S(2)}, u32[]{:S(2)}) %collective-permute-start.22) | collective-permute-done | bytes 458784 | tf_op jit(solution)/shard_map/ppermute | solution.py:21
  48.9 1.0 %combine.1 = bf16[128,1792]{1,0:T(8,128)(2,1)} custom-call(bf16[128,256]{1,0:T(8,128)(2,1)S(1)} %get-tuple-element.34.place_ref, f32[128,1792]{1,0:T(8,128)S(1)} %get-tuple-element.44.base_ref, bf16[128,1792]{1,0:T(8,128)(2,1)S(1)} %collective-permute-done.22.mate_ref, bf16[32,1792]{1,0:T(8,128)(2,1)S(1)} %get-tuple-element.45.refs_0_, ...), custom_call_target="tpu_custom_call" | custom-call | flops 8388608 | bytes 917504 | tf_op jit(solution)/shard_map/combine/pallas_call | solution.py:252
  (19 shorter events, 0.1 us)
Async XLA Ops:
  0.0 4.4 %collective-permute-start = (bf16[8,8192]{1,0:T(8,128)(2,1)}, bf16[8,8192]{1,0:T(8,128)(2,1)S(1)}, u32[]{:S(2)}, u32[]{:S(2)}) collective-permute-start(bf16[8,8192]{1,0:T(8,128)(2,1)} %refs_0_.1), channel_id=1, source_target_pairs={{0,1},{1,0},{2,3},{3,2},{4,5},{5,4},{6,7},{7,6},{8,9},{9,8},{10,11... | collective-permute-start | bytes 393224 | tf_op jit(solution)/shard_map/ppermute | solution.py:21
  0.7 10.4 %collective-permute-start.7 = (bf16[8,8192]{1,0:T(8,128)(2,1)}, bf16[8,8192]{1,0:T(8,128)(2,1)S(1)}, u32[]{:S(2)}, u32[]{:S(2)}) collective-permute-start(bf16[8,8192]{1,0:T(8,128)(2,1)} %refs_0_.1), channel_id=1, source_target_pairs={{0,8},{1,9},{2,10},{3,11},{4,12},{5,13},{6,14},{7,15},{8,0},{9,1},... | collective-permute-start | bytes 393224 | tf_op jit(solution)/shard_map/ppermute | solution.py:21
  3.0 6.9 %collective-permute-start.3 = (bf16[8,8192]{1,0:T(8,128)(2,1)}, bf16[8,8192]{1,0:T(8,128)(2,1)S(1)}, u32[]{:S(2)}, u32[]{:S(2)}) collective-permute-start(bf16[8,8192]{1,0:T(8,128)(2,1)} %refs_0_.1), channel_id=1, source_target_pairs={{0,4},{1,5},{2,6},{3,7},{4,0},{5,1},{6,2},{7,3},{8,12},{9,13},{10,... | collective-permute-start | bytes 393224 | tf_op jit(solution)/shard_map/ppermute | solution.py:21
  3.2 9.4 %collective-permute-start.1 = (bf16[8,8192]{1,0:T(8,128)(2,1)}, bf16[8,8192]{1,0:T(8,128)(2,1)S(1)}, u32[]{:S(2)}, u32[]{:S(2)}) collective-permute-start(bf16[8,8192]{1,0:T(8,128)(2,1)} %refs_0_.1), channel_id=1, source_target_pairs={{0,2},{1,3},{2,0},{3,1},{4,6},{5,7},{6,4},{7,5},{8,10},{9,11},{10,... | collective-permute-start | bytes 393224 | tf_op jit(solution)/shard_map/ppermute | solution.py:21
  4.4 10.5 %collective-permute-start.11 = (bf16[8,8192]{1,0:T(8,128)(2,1)}, bf16[8,8192]{1,0:T(8,128)(2,1)S(1)}, u32[]{:S(2)}, u32[]{:S(2)}) collective-permute-start(bf16[8,8192]{1,0:T(8,128)(2,1)} %refs_0_.1), channel_id=1, source_target_pairs={{0,12},{1,13},{2,14},{3,15},{4,8},{5,9},{6,10},{7,11},{8,4},{9,5},... | collective-permute-start | bytes 393224 | tf_op jit(solution)/shard_map/ppermute | solution.py:21
  4.5 0.7 %copy-start.2 = (s32[128,1]{0,1:T(1,128)S(1)}, s32[128,1]{0,1:T(1,128)}, u32[]{:S(2)}) copy-start(s32[128,1]{0,1:T(1,128)} %param.11) | copy-start | bytes 1540
  5.2 1.2 %copy-start.3 = (bf16[1,8192,64]{1,2,0:T(8,128)(2,1)S(1)}, bf16[1,8192,64]{1,2,0:T(8,128)(2,1)}, u32[]{:S(2)}) copy-start(bf16[1,8192,64]{1,2,0:T(8,128)(2,1)} %param.8) | copy-start | bytes 3145732
  6.4 16.2 %copy-start = (bf16[1,64,28672]{2,1,0:T(8,128)(2,1)S(1)}, bf16[1,64,28672]{2,1,0:T(8,128)(2,1)}, u32[]{:S(2)}) copy-start(bf16[1,64,28672]{2,1,0:T(8,128)(2,1)} %param.9) | copy-start | bytes 11010052
  6.4 16.2 %copy-start.1 = (bf16[8,8192]{1,0:T(8,128)(2,1)S(1)}, bf16[8,8192]{1,0:T(8,128)(2,1)}, u32[]{:S(2)}) copy-start(bf16[8,8192]{1,0:T(8,128)(2,1)} %refs_0_.1) | copy-start | bytes 393220
  9.9 6.2 %collective-permute-start.5 = (bf16[8,8192]{1,0:T(8,128)(2,1)S(1)}, bf16[8,8192]{1,0:T(8,128)(2,1)S(1)}, u32[]{:S(2)}, u32[]{:S(2)}) collective-permute-start(bf16[8,8192]{1,0:T(8,128)(2,1)S(1)} %collective-permute-done.3.refs_4_), channel_id=1, source_target_pairs={{0,2},{1,3},{2,0},{3,1},{4,6},{5,7},{6,4},{7,5},{8,10},{9,11},{10,... | collective-permute-start | bytes 393224 | tf_op jit(solution)/shard_map/ppermute | solution.py:21
  11.1 5.7 %collective-permute-start.4 = (bf16[8,8192]{1,0:T(8,128)(2,1)S(1)}, bf16[8,8192]{1,0:T(8,128)(2,1)S(1)}, u32[]{:S(2)}, u32[]{:S(2)}) collective-permute-start(bf16[8,8192]{1,0:T(8,128)(2,1)S(1)} %collective-permute-done.3.refs_4_), channel_id=1, source_target_pairs={{0,1},{1,0},{2,3},{3,2},{4,5},{5,4},{6,7},{7,6},{8,9},{9,8},{10,11... | collective-permute-start | bytes 393224 | tf_op jit(solution)/shard_map/ppermute | solution.py:21
  12.5 4.4 %collective-permute-start.2 = (bf16[8,8192]{1,0:T(8,128)(2,1)S(1)}, bf16[8,8192]{1,0:T(8,128)(2,1)S(1)}, u32[]{:S(2)}, u32[]{:S(2)}) collective-permute-start(bf16[8,8192]{1,0:T(8,128)(2,1)S(1)} %collective-permute-done.1.refs_2_), channel_id=1, source_target_pairs={{0,1},{1,0},{2,3},{3,2},{4,5},{5,4},{6,7},{7,6},{8,9},{9,8},{10,11... | collective-permute-start | bytes 393224 | tf_op jit(solution)/shard_map/ppermute | solution.py:21
  12.6 5.2 %collective-permute-start.9 = (bf16[8,8192]{1,0:T(8,128)(2,1)S(1)}, bf16[8,8192]{1,0:T(8,128)(2,1)S(1)}, u32[]{:S(2)}, u32[]{:S(2)}) collective-permute-start(bf16[8,8192]{1,0:T(8,128)(2,1)S(1)} %collective-permute-done.7.refs_8_), channel_id=1, source_target_pairs={{0,2},{1,3},{2,0},{3,1},{4,6},{5,7},{6,4},{7,5},{8,10},{9,11},{10,... | collective-permute-start | bytes 393224 | tf_op jit(solution)/shard_map/ppermute | solution.py:21
  14.9 5.8 %collective-permute-start.13 = (bf16[8,8192]{1,0:T(8,128)(2,1)S(1)}, bf16[8,8192]{1,0:T(8,128)(2,1)S(1)}, u32[]{:S(2)}, u32[]{:S(2)}) collective-permute-start(bf16[8,8192]{1,0:T(8,128)(2,1)S(1)} %collective-permute-done.11.refs_12_), channel_id=1, source_target_pairs={{0,2},{1,3},{2,0},{3,1},{4,6},{5,7},{6,4},{7,5},{8,10},{9,11},{10,... | collective-permute-start | bytes 393224 | tf_op jit(solution)/shard_map/ppermute | solution.py:21
  16.1 6.2 %collective-permute-start.8 = (bf16[8,8192]{1,0:T(8,128)(2,1)S(1)}, bf16[8,8192]{1,0:T(8,128)(2,1)S(1)}, u32[]{:S(2)}, u32[]{:S(2)}) collective-permute-start(bf16[8,8192]{1,0:T(8,128)(2,1)S(1)} %collective-permute-done.7.refs_8_), channel_id=1, source_target_pairs={{0,1},{1,0},{2,3},{3,2},{4,5},{5,4},{6,7},{7,6},{8,9},{9,8},{10,11... | collective-permute-start | bytes 393224 | tf_op jit(solution)/shard_map/ppermute | solution.py:21
  16.8 5.5 %collective-permute-start.12 = (bf16[8,8192]{1,0:T(8,128)(2,1)S(1)}, bf16[8,8192]{1,0:T(8,128)(2,1)S(1)}, u32[]{:S(2)}, u32[]{:S(2)}) collective-permute-start(bf16[8,8192]{1,0:T(8,128)(2,1)S(1)} %collective-permute-done.11.refs_12_), channel_id=1, source_target_pairs={{0,1},{1,0},{2,3},{3,2},{4,5},{5,4},{6,7},{7,6},{8,9},{9,8},{10,11... | collective-permute-start | bytes 393224 | tf_op jit(solution)/shard_map/ppermute | solution.py:21
  16.9 5.4 %collective-permute-start.6 = (bf16[8,8192]{1,0:T(8,128)(2,1)S(1)}, bf16[8,8192]{1,0:T(8,128)(2,1)S(1)}, u32[]{:S(2)}, u32[]{:S(2)}) collective-permute-start(bf16[8,8192]{1,0:T(8,128)(2,1)S(1)} %collective-permute-done.5.refs_6_), channel_id=1, source_target_pairs={{0,1},{1,0},{2,3},{3,2},{4,5},{5,4},{6,7},{7,6},{8,9},{9,8},{10,11... | collective-permute-start | bytes 393224 | tf_op jit(solution)/shard_map/ppermute | solution.py:21
  17.8 4.5 %collective-permute-start.10 = (bf16[8,8192]{1,0:T(8,128)(2,1)S(1)}, bf16[8,8192]{1,0:T(8,128)(2,1)S(1)}, u32[]{:S(2)}, u32[]{:S(2)}) collective-permute-start(bf16[8,8192]{1,0:T(8,128)(2,1)S(1)} %collective-permute-done.9.refs_10_), channel_id=1, source_target_pairs={{0,1},{1,0},{2,3},{3,2},{4,5},{5,4},{6,7},{7,6},{8,9},{9,8},{10,11... | collective-permute-start | bytes 393224 | tf_op jit(solution)/shard_map/ppermute | solution.py:21
  20.6 2.0 %collective-permute-start.14 = (bf16[8,8192]{1,0:T(8,128)(2,1)S(1)}, bf16[8,8192]{1,0:T(8,128)(2,1)S(1)}, u32[]{:S(2)}, u32[]{:S(2)}) collective-permute-start(bf16[8,8192]{1,0:T(8,128)(2,1)S(1)} %collective-permute-done.13.refs_14_), channel_id=1, source_target_pairs={{0,1},{1,0},{2,3},{3,2},{4,5},{5,4},{6,7},{7,6},{8,9},{9,8},{10,11... | collective-permute-start | bytes 393224 | tf_op jit(solution)/shard_map/ppermute | solution.py:21
  23.7 5.5 %collective-permute-start.17 = (bf16[32,1792]{1,0:T(8,128)(2,1)S(1)}, bf16[32,1792]{1,0:T(8,128)(2,1)S(1)}, u32[]{:S(2)}, u32[]{:S(2)}) collective-permute-start(bf16[32,1792]{1,0:T(8,128)(2,1)S(1)} %get-tuple-element.38), channel_id=1, source_target_pairs={{0,8},{1,9},{2,10},{3,11},{4,12},{5,13},{6,14},{7,15},{8,0},{9,1},... | collective-permute-start | bytes 344072 | tf_op jit(solution)/shard_map/ppermute | solution.py:21
  24.7 6.6 %collective-permute-start.15 = (bf16[32,1792]{1,0:T(8,128)(2,1)S(1)}, bf16[32,1792]{1,0:T(8,128)(2,1)S(1)}, u32[]{:S(2)}, u32[]{:S(2)}) collective-permute-start(bf16[32,1792]{1,0:T(8,128)(2,1)S(1)} %get-tuple-element.36), channel_id=1, source_target_pairs={{0,2},{1,3},{2,0},{3,1},{4,6},{5,7},{6,4},{7,5},{8,10},{9,11},{10,... | collective-permute-start | bytes 344072 | tf_op jit(solution)/shard_map/ppermute | solution.py:21
  25.8 18.5 %collective-permute-start.16 = (bf16[32,1792]{1,0:T(8,128)(2,1)S(1)}, bf16[32,1792]{1,0:T(8,128)(2,1)S(1)}, u32[]{:S(2)}, u32[]{:S(2)}) collective-permute-start(bf16[32,1792]{1,0:T(8,128)(2,1)S(1)} %get-tuple-element.37), channel_id=1, source_target_pairs={{0,4},{1,5},{2,6},{3,7},{4,0},{5,1},{6,2},{7,3},{8,12},{9,13},{10,... | collective-permute-start | bytes 344072 | tf_op jit(solution)/shard_map/ppermute | solution.py:21
  28.0 16.3 %collective-permute-start.18 = (bf16[32,1792]{1,0:T(8,128)(2,1)S(1)}, bf16[32,1792]{1,0:T(8,128)(2,1)S(1)}, u32[]{:S(2)}, u32[]{:S(2)}) collective-permute-start(bf16[32,1792]{1,0:T(8,128)(2,1)S(1)} %get-tuple-element.39), channel_id=1, source_target_pairs={{0,10},{1,11},{2,8},{3,9},{4,14},{5,15},{6,12},{7,13},{8,2},{9,3},... | collective-permute-start | bytes 344072 | tf_op jit(solution)/shard_map/ppermute | solution.py:21
  28.0 16.3 %collective-permute-start.19 = (bf16[32,1792]{1,0:T(8,128)(2,1)S(1)}, bf16[32,1792]{1,0:T(8,128)(2,1)S(1)}, u32[]{:S(2)}, u32[]{:S(2)}) collective-permute-start(bf16[32,1792]{1,0:T(8,128)(2,1)S(1)} %get-tuple-element.40), channel_id=1, source_target_pairs={{0,12},{1,13},{2,14},{3,15},{4,8},{5,9},{6,10},{7,11},{8,4},{9,5},... | collective-permute-start | bytes 344072 | tf_op jit(solution)/shard_map/ppermute | solution.py:21
  29.2 17.1 %collective-permute-start.20 = (bf16[32,1792]{1,0:T(8,128)(2,1)S(1)}, bf16[32,1792]{1,0:T(8,128)(2,1)S(1)}, u32[]{:S(2)}, u32[]{:S(2)}) collective-permute-start(bf16[32,1792]{1,0:T(8,128)(2,1)S(1)} %get-tuple-element.41), channel_id=1, source_target_pairs={{0,14},{1,15},{2,12},{3,13},{4,10},{5,11},{6,8},{7,9},{8,6},{9,7},... | collective-permute-start | bytes 344072 | tf_op jit(solution)/shard_map/ppermute | solution.py:21
  31.2 15.1 %collective-permute-start.21 = (bf16[32,1792]{1,0:T(8,128)(2,1)S(1)}, bf16[32,1792]{1,0:T(8,128)(2,1)S(1)}, u32[]{:S(2)}, u32[]{:S(2)}) collective-permute-start(bf16[32,1792]{1,0:T(8,128)(2,1)S(1)} %get-tuple-element.42), channel_id=1, source_target_pairs={{0,6},{1,7},{2,4},{3,5},{4,2},{5,3},{6,0},{7,1},{8,14},{9,15},{10,... | collective-permute-start | bytes 344072 | tf_op jit(solution)/shard_map/ppermute | solution.py:21
  46.4 2.5 %collective-permute-start.22 = (bf16[128,1792]{1,0:T(8,128)(2,1)S(1)}, bf16[128,1792]{1,0:T(8,128)(2,1)S(1)}, u32[]{:S(2)}, u32[]{:S(2)}) collective-permute-start(bf16[128,1792]{1,0:T(8,128)(2,1)S(1)} %slice_dynamic-update-slice_fusion), channel_id=1, source_target_pairs={{0,1},{1,0},{2,3},{3,2},{4,5},{5,4},{6,7},{7,6},{8,9},{9,8},{10,11... | collective-permute-start | bytes 1376264 | tf_op jit(solution)/shard_map/ppermute | solution.py:21
